TPU v7x, 256 devices: a whole 4x4x8 slice. The times are simulated.
256 devices in a mesh: seq: 32 (over x, z), head: 8 (over y, core).
Axes of the slice: x: 4, y: 4, z: 8, core: 2. Of those that a mesh axis runs over, the one named last changes fastest.
Arguments:
- queries: bfloat16 [16384, 4096], P('seq', 'head'), may hold values from -6 to 6
- key_inputs: bfloat16 [16384, 4096], P('seq', 'head'), may hold values from -6 to 6
- value_inputs: bfloat16 [16384, 4096], P('seq', 'head'), may hold values from -6 to 6
- head_scale: float32 [32], P('head'), may hold values from 0.25 to 4
- out_gain: float32 [4096], P('head'), may hold values from 0.5 to 1.5
Outputs:
- layer_out: bfloat16 [16384, 4096], P('seq', 'head')
All inputs are finite; a program needn't handle non-finite values.
Results may differ from a plain program's by a relative error of at most 0.008.
Values may be sent and summed in bfloat16 or wider, within the bound.
A program may use at most 64 MiB of HBM per device.

v0:
```python
import jax
import jax.numpy as jnp
from jax import lax
from jax.sharding import PartitionSpec as P

BLOCK = 128
LEVELS = 7


EPSILON = 1e-06


def from_behind(block, axis, distance):
    devices = range(lax.axis_size(axis))
    route = [(i - distance, i) for i in devices if i - distance in devices]
    return lax.ppermute(block, axis, route)


def extended_2(x, sides, width):
    for axis, dim in sides:
        size, length = (lax.axis_size(axis), x.shape[dim])
        up = [(i, (i + 1) % size) for i in range(size - 1)]
        down = [(j, i) for i, j in up]
        last = lax.slice_in_dim(x, length - width, length, axis=dim)
        initial = lax.slice_in_dim(x, 0, width, axis=dim)
        before = lax.ppermute(last, axis, up)
        after = lax.ppermute(initial, axis, down)
        x = jnp.concatenate([before, x, after], axis=dim)
    return x


def from_partner(x, axis, bit):
    return lax.ppermute(x, axis, [(i, i ^ 1 << bit) for i in range(lax.axis_size(axis))])


def unit_heads(matrix, head_count, head_width):
    tensor = matrix.reshape(matrix.shape[0], head_count, head_width).astype(jnp.float32)
    inverse = lax.rsqrt(jnp.mean(tensor * tensor, axis=-1, keepdims=True) + EPSILON)
    return (tensor * inverse).astype(jnp.bfloat16)


def pair_sums(tensor):
    pair_count = tensor.shape[0] // 2
    grouped = tensor.reshape(pair_count, 2, tensor.shape[1], tensor.shape[2]).astype(jnp.float32)
    return jnp.sum(grouped, axis=1)


def half_masks(positions, block_rows):
    half_rows = block_rows // 2
    query_half = positions // half_rows
    key_half = jnp.arange(block_rows) // half_rows
    before = query_half[:, None] >= key_half[None, :]
    after = key_half[None, :] >= query_half[:, None]
    return (before, after)


def attend(query_tiles, key_blocks, value_blocks, allowed, weight, head_width):
    attention_logits = jnp.einsum(
        "bqhe,bkhe->bhqk", query_tiles, key_blocks, preferred_element_type=jnp.float32
    ) * head_width ** (-0.5)
    weights = jnp.where(allowed[:, None], jnp.exp(attention_logits), 0.0)
    totals = weight * jnp.sum(weights, axis=-1)
    mixed_output = weight * jnp.einsum(
        "bhqk,bkhe->bqhe",
        weights.astype(jnp.bfloat16),
        value_blocks,
        preferred_element_type=jnp.float32,
    )
    return (mixed_output, jnp.swapaxes(totals, 1, 2))


def near_terms(coarse_queries, extended, level_index, seq_place, seq_count, block_rows):
    coarse_rows, head_count, head_width = coarse_queries.shape
    local_blocks = coarse_rows // block_rows
    block_shape = (2, local_blocks, block_rows, head_count, head_width)
    before_blocks = extended[:, :coarse_rows].reshape(block_shape)
    after_blocks = extended[:, 2 * block_rows :].reshape(block_shape)
    numbers = seq_place * local_blocks + jnp.arange(local_blocks)
    before_ok = (numbers >= 1)[:, None, None]
    after_ok = (numbers <= seq_count * local_blocks - 2)[:, None, None]
    if level_index == 0:
        centre = extended[:, block_rows : block_rows + coarse_rows].reshape(block_shape)
        windows = jnp.concatenate([before_blocks, centre, after_blocks], axis=2)
        square = (local_blocks, block_rows, block_rows)
        allowed = jnp.concatenate(
            [
                jnp.broadcast_to(before_ok, square),
                jnp.ones(square, jnp.bool_),
                jnp.broadcast_to(after_ok, square),
            ],
            axis=2,
        )
    else:
        windows = jnp.concatenate([before_blocks, after_blocks], axis=2)
        before, after = half_masks(jnp.arange(block_rows), block_rows)
        allowed = jnp.concatenate([before_ok & before[None], after_ok & after[None]], axis=2)
    query_tiles = coarse_queries.reshape(local_blocks, block_rows, head_count, head_width)
    mixed_output, totals = attend(
        query_tiles, windows[0], windows[1], allowed, 2.0**level_index, head_width
    )
    return (
        mixed_output.reshape(coarse_rows, head_count, head_width),
        totals.reshape(coarse_rows, head_count),
    )


def far_terms(
    coarse_queries, before_block, after_block, level_index, seq_place, seq_count, block_rows
):
    coarse_rows, head_count, head_width = coarse_queries.shape
    group_size = block_rows // coarse_rows
    number = seq_place // group_size
    positions = seq_place % group_size * coarse_rows + jnp.arange(coarse_rows)
    before, after = half_masks(positions, block_rows)
    before = before & (number >= 1)
    after = after & (number <= seq_count // group_size - 2)
    allowed = jnp.concatenate([before, after], axis=1)[None]
    windows = jnp.concatenate([before_block, after_block], axis=1)
    mixed_output, totals = attend(
        coarse_queries[None],
        windows[0][None],
        windows[1][None],
        allowed,
        2.0**level_index,
        head_width,
    )
    return (mixed_output[0], totals[0])


def spread_add(numerator, denominator, mixed_output, totals, level_index):
    repeat_factor = 2**level_index
    row_count, head_count, head_width = numerator.shape
    coarse_rows = row_count // repeat_factor
    numerator = (
        numerator.reshape(coarse_rows, repeat_factor, head_count, head_width)
        + mixed_output[:, None]
    ).reshape(row_count, head_count, head_width)
    denominator = (
        denominator.reshape(coarse_rows, repeat_factor, head_count) + totals[:, None]
    ).reshape(row_count, head_count)
    return (numerator, denominator)


def neighbour_block(gathered_block, distance):
    return from_behind(gathered_block, "seq", distance)


def on_device(queries, key_inputs, value_inputs, head_scale, out_gain):
    row_count = queries.shape[0]
    head_count = head_scale.shape[0]
    head_width = queries.shape[1] // head_count
    block_rows = BLOCK
    seq_count = lax.axis_size("seq")
    seq_place = lax.axis_index("seq")
    query_unit = unit_heads(queries, head_count, head_width)
    key_unit = unit_heads(key_inputs, head_count, head_width)
    value_heads = value_inputs.reshape(row_count, head_count, head_width)
    near_levels = []
    far_levels = []
    pooled_sums = (query_unit, key_unit, value_heads)
    for level_index in range(LEVELS):
        if level_index == 0:
            coarse = pooled_sums
        else:
            pooled_sums = tuple((pair_sums(tensor) for tensor in pooled_sums))
            coarse = tuple(
                ((tensor * 0.5**level_index).astype(jnp.bfloat16) for tensor in pooled_sums)
            )
        paired = jnp.stack([coarse[1], coarse[2]])
        if coarse[0].shape[0] >= block_rows:
            near_levels.append((level_index, coarse[0], paired))
        else:
            far_levels.append((level_index, coarse[0], paired))
    numerator = jnp.zeros((row_count, head_count, head_width), jnp.float32)
    denominator = jnp.zeros((row_count, head_count), jnp.float32)
    extended_list = []
    for level_index, coarse_queries, paired in near_levels:
        extended_list.append(extended_2(paired, (("seq", 1),), block_rows))
    for entry, extended in zip(near_levels, extended_list):
        level_index, coarse_queries, paired = entry
        mixed_output, totals = near_terms(
            coarse_queries, extended, level_index, seq_place, seq_count, block_rows
        )
        numerator, denominator = spread_add(
            numerator, denominator, mixed_output, totals, level_index
        )
    for level_index, coarse_queries, paired in far_levels:
        coarse_rows = paired.shape[1]
        group_size = block_rows // coarse_rows
        gathered_block = paired
        for bit_index in range(group_size.bit_length() - 1):
            partner = from_partner(gathered_block, "seq", bit_index)
            lower_half = seq_place // 2**bit_index % 2 == 0
            gathered_block = jnp.where(
                lower_half,
                jnp.concatenate([gathered_block, partner], axis=1),
                jnp.concatenate([partner, gathered_block], axis=1),
            )
        before_block = neighbour_block(gathered_block, group_size)
        after_block = neighbour_block(gathered_block, -group_size)
        mixed_output, totals = far_terms(
            coarse_queries, before_block, after_block, level_index, seq_place, seq_count, block_rows
        )
        numerator, denominator = spread_add(
            numerator, denominator, mixed_output, totals, level_index
        )
    attended = numerator / denominator[:, :, None]
    scaled = attended * head_scale[None, :, None]
    token_total = lax.psum(jnp.sum(scaled * scaled, axis=(1, 2)), "head")
    model_width = head_count * head_width * lax.axis_size("head")
    factor = lax.rsqrt(token_total / model_width + EPSILON)
    normed = (scaled * factor[:, None, None]).reshape(
        row_count, head_count * head_width
    ) * out_gain[None, :]
    return normed.astype(jnp.bfloat16)


def solution(mesh):
    placed = (P("seq", "head"), P("seq", "head"), P("seq", "head"), P("head"), P("head"))
    return jax.shard_map(
        on_device, mesh=mesh, in_specs=placed, out_specs=P("seq", "head"), check_vma=False
    )
```

profile of v0, /device:TPU:1, one launch (start us, length us, event | category | flops | bytes accessed | tf_op | source)
XLA Modules:
  0.0 223.8 jit_solution(1620741578211440096)
XLA Ops:
  4.4 1.3 reshape.971
  5.7 1.8 reduce_sum.257
  8.4 2.5 %collective-permute-start.6 = (bf16[2,64,4,128]{3,1,2,0:T(8,128)(2,1)}, bf16[2,64,4,128]{3,1,2,0:T(8,128)(2,1)}, u32[]{:S(2)}, u32[]{:S(2)}) collective-permute-start(bf16[2,64,4,128]{3,1,2,0:T(8,128)(2,1)} %pad_maximum_fusion.14), channel_id=1, source_target_pairs={{0,8},{8,0},{16,24},{24,16},{32,40},{40,32},{48,56},{56,48},{64,72... | collective-permute-start | bytes 393224 | tf_op jit(solution)/shard_map/ppermute | solution.py:33
  12.3 1.5 collective-permute-start.13
  15.3 4.0 %collective-permute-start.4 = (bf16[2,128,4,128]{3,1,2,0:T(8,128)(2,1)}, bf16[2,128,4,128]{3,1,2,0:T(8,128)(2,1)}, u32[]{:S(2)}, u32[]{:S(2)}) collective-permute-start(bf16[2,128,4,128]{3,1,2,0:T(8,128)(2,1)} %pad_maximum_fusion.13), channel_id=1, source_target_pairs={{0,8},{8,16},{16,24},{24,32},{32,40},{40,48},{48,56},{56,64},{64,7... | collective-permute-start | bytes 786440 | tf_op jit(solution)/shard_map/ppermute | solution.py:26
  21.0 1.3 reshape.972
  24.4 2.5 %mul.501 = f32[512,4,128]{2,1,0:T(4,128)} reshape(f32[512,512]{1,0:T(8,128)} %convert_multiply_fusion) | data formatting | bytes 2097152 | tf_op jit(solution)/shard_map/mul | solution.py:38
  27.0 1.9 reduce_sum.255
  31.7 1.3 reshape.973
  37.0 1.4 broadcast_compare_fusion.1
  39.3 1.6 copy.409
  40.9 1.3 broadcast_bitcast_fusion
  46.1 2.3 %pad_maximum_fusion.10 = (bf16[2,128,4,128]{3,2,1,0:T(4,128)(2,1)}, bf16[2,128,4,128]{3,2,1,0:T(4,128)(2,1)}) fusion(bf16[1,256,4,128]{3,2,1,0:T(4,128)(2,1)} %get-tuple-element.52, bf16[1,256,4,128]{3,2,1,0:T(4,128)(2,1)} %get-tuple-element.51), kind=kLoop, calls=%fused_computation.113 | loop fusion | flops 262144 | bytes 1048576 | tf_op jit(solution)/shard_map/stack | solution.py:169
  52.3 1.8 multiply_convert_fusion.2
  56.6 1.3 reshape.969
  58.8 3.1 %collective-permute-start = (bf16[2,128,4,128]{1,3,2,0:T(8,128)(2,1)}, bf16[2,128,4,128]{1,3,2,0:T(8,128)(2,1)S(1)}, u32[]{:S(2)}, u32[]{:S(2)}) collective-permute-start(bf16[2,128,4,128]{1,3,2,0:T(8,128)(2,1)} %get-tuple-element.7), channel_id=1, source_target_pairs={{0,8},{8,16},{16,24},{24,32},{32,40},{40,48},{48,56},{56,64},{64,7... | collective-permute-start | bytes 786440 | tf_op jit(solution)/shard_map/ppermute | solution.py:26
  62.7 4.3 %collective-permute-start.19 = (bf16[2,16,4,128]{3,1,2,0:T(8,128)(2,1)S(1)}, bf16[2,16,4,128]{3,1,2,0:T(8,128)(2,1)S(1)}, u32[]{:S(2)}, u32[]{:S(2)}) collective-permute-start(bf16[2,16,4,128]{3,1,2,0:T(8,128)(2,1)S(1)} %maximum_select_fusion.9), channel_id=1, source_target_pairs={{0,16},{8,24},{16,0},{24,8},{32,48},{40,56},{48,32},{56,40},{64,80... | collective-permute-start | bytes 98312 | tf_op jit(solution)/shard_map/ppermute | solution.py:33
  69.6 3.5 %collective-permute-start.14 = (bf16[2,32,4,128]{3,1,2,0:T(8,128)(2,1)S(1)}, bf16[2,32,4,128]{3,1,2,0:T(8,128)(2,1)S(1)}, u32[]{:S(2)}, u32[]{:S(2)}) collective-permute-start(bf16[2,32,4,128]{3,1,2,0:T(8,128)(2,1)S(1)} %maximum_select_fusion.7), channel_id=1, source_target_pairs={{0,16},{8,24},{16,0},{24,8},{32,48},{40,56},{48,32},{56,40},{64,80... | collective-permute-start | bytes 196616 | tf_op jit(solution)/shard_map/ppermute | solution.py:33
  74.1 3.5 %collective-permute-done.14 = bf16[2,32,4,128]{3,1,2,0:T(8,128)(2,1)S(1)} collective-permute-done((bf16[2,32,4,128]{3,1,2,0:T(8,128)(2,1)S(1)}, bf16[2,32,4,128]{3,1,2,0:T(8,128)(2,1)S(1)}, u32[]{:S(2)}, u32[]{:S(2)}) %collective-permute-start.14) | collective-permute-done | bytes 65568 | tf_op jit(solution)/shard_map/ppermute | solution.py:33
  77.6 2.8 %collective-permute-start.20 = (bf16[2,32,4,128]{3,1,2,0:T(8,128)(2,1)S(1)}, bf16[2,32,4,128]{3,1,2,0:T(8,128)(2,1)S(1)}, u32[]{:S(2)}, u32[]{:S(2)}) collective-permute-start(bf16[2,32,4,128]{3,1,2,0:T(8,128)(2,1)S(1)} %maximum_select_fusion.8), channel_id=1, source_target_pairs={{0,32},{8,40},{16,48},{24,56},{32,0},{40,8},{48,16},{56,24},{64,96... | collective-permute-start | bytes 196616 | tf_op jit(solution)/shard_map/ppermute | solution.py:33
  80.5 4.9 %collective-permute-done.20 = bf16[2,32,4,128]{3,1,2,0:T(8,128)(2,1)S(1)} collective-permute-done((bf16[2,32,4,128]{3,1,2,0:T(8,128)(2,1)S(1)}, bf16[2,32,4,128]{3,1,2,0:T(8,128)(2,1)S(1)}, u32[]{:S(2)}, u32[]{:S(2)}) %collective-permute-start.20) | collective-permute-done | bytes 65568 | tf_op jit(solution)/shard_map/ppermute | solution.py:33
  85.4 2.2 %collective-permute-start.15 = (bf16[2,64,4,128]{3,1,2,0:T(8,128)(2,1)S(1)}, bf16[2,64,4,128]{3,1,2,0:T(8,128)(2,1)S(1)}, u32[]{:S(2)}, u32[]{:S(2)}) collective-permute-start(bf16[2,64,4,128]{3,1,2,0:T(8,128)(2,1)S(1)} %maximum_select_fusion.5), channel_id=1, source_target_pairs={{0,32},{8,40},{16,48},{24,56},{32,0},{40,8},{48,16},{56,24},{64,96... | collective-permute-start | bytes 393224 | tf_op jit(solution)/shard_map/ppermute | solution.py:33
  87.6 1.8 maximum_select_fusion
  89.4 2.5 %collective-permute-done.10 = bf16[2,64,4,128]{3,1,2,0:T(8,128)(2,1)S(1)} collective-permute-done((bf16[2,64,4,128]{3,1,2,0:T(8,128)(2,1)S(1)}, bf16[2,64,4,128]{3,1,2,0:T(8,128)(2,1)S(1)}, u32[]{:S(2)}, u32[]{:S(2)}) %collective-permute-start.10) | collective-permute-done | bytes 131104 | tf_op jit(solution)/shard_map/ppermute | solution.py:33
  91.9 5.0 %collective-permute-start.21 = (bf16[2,64,4,128]{3,1,2,0:T(8,128)(2,1)S(1)}, bf16[2,64,4,128]{3,1,2,0:T(8,128)(2,1)S(1)}, u32[]{:S(2)}, u32[]{:S(2)}) collective-permute-start(bf16[2,64,4,128]{3,1,2,0:T(8,128)(2,1)S(1)} %maximum_select_fusion.6), channel_id=1, source_target_pairs={{0,64},{8,72},{16,80},{24,88},{32,96},{40,104},{48,112},{56,120},{... | collective-permute-start | bytes 393224 | tf_op jit(solution)/shard_map/ppermute | solution.py:33
  97.8 1.3 collective-permute-start.5
  99.8 4.7 %collective-permute-start.2 = (bf16[2,128,4,128]{3,2,1,0:T(4,128)(2,1)}, bf16[2,128,4,128]{3,2,1,0:T(4,128)(2,1)}, u32[]{:S(2)}, u32[]{:S(2)}) collective-permute-start(bf16[2,128,4,128]{3,2,1,0:T(4,128)(2,1)} %get-tuple-element.12), channel_id=1, source_target_pairs={{0,8},{8,16},{16,24},{24,32},{32,40},{40,48},{48,56},{56,64},{64,7... | collective-permute-start | bytes 786440 | tf_op jit(solution)/shard_map/ppermute | solution.py:26
  106.6 3.8 %collective-permute-start.7 = (bf16[2,128,4,128]{3,1,2,0:T(8,128)(2,1)}, bf16[2,128,4,128]{3,1,2,0:T(8,128)(2,1)}, u32[]{:S(2)}, u32[]{:S(2)}) collective-permute-start(bf16[2,128,4,128]{3,1,2,0:T(8,128)(2,1)} %maximum_select_fusion), channel_id=1, source_target_pairs={{0,16},{8,24},{16,32},{24,40},{32,48},{40,56},{48,64},{56,72},{64,... | collective-permute-start | bytes 786440 | tf_op jit(solution)/shard_map/ppermute | solution.py:16
  112.0 1.4 pad_maximum_fusion
  113.5 1.3 fusion
  115.6 1.3 collective-permute-start.8
  116.9 8.9 %collective-permute-start.11 = (bf16[2,128,4,128]{3,1,2,0:T(8,128)(2,1)}, bf16[2,128,4,128]{3,1,2,0:T(8,128)(2,1)}, u32[]{:S(2)}, u32[]{:S(2)}) collective-permute-start(bf16[2,128,4,128]{3,1,2,0:T(8,128)(2,1)} %maximum_select_fusion.1), channel_id=1, source_target_pairs={{0,32},{8,40},{16,48},{24,56},{32,64},{40,72},{48,80},{56,88},{64,... | collective-permute-start | bytes 786440 | tf_op jit(solution)/shard_map/ppermute | solution.py:16
  125.8 1.9 fusion.117
  133.3 1.3 collective-permute-start.12
  134.6 9.2 %collective-permute-start.16 = (bf16[2,128,4,128]{3,1,2,0:T(8,128)(2,1)}, bf16[2,128,4,128]{3,1,2,0:T(8,128)(2,1)}, u32[]{:S(2)}, u32[]{:S(2)}) collective-permute-start(bf16[2,128,4,128]{3,1,2,0:T(8,128)(2,1)} %maximum_select_fusion.2), channel_id=1, source_target_pairs={{0,64},{8,72},{16,80},{24,88},{32,96},{40,104},{48,112},{56,120},{... | collective-permute-start | bytes 786440 | tf_op jit(solution)/shard_map/ppermute | solution.py:16
  143.8 1.9 pad_maximum_fusion.5
  146.9 1.4 fusion.118
  150.3 1.3 fusion.13
  152.7 1.3 collective-permute-start.17
  155.0 5.7 %collective-permute-start.22 = (bf16[2,128,4,128]{3,1,2,0:T(8,128)(2,1)}, bf16[2,128,4,128]{3,1,2,0:T(8,128)(2,1)}, u32[]{:S(2)}, u32[]{:S(2)}) collective-permute-start(bf16[2,128,4,128]{3,1,2,0:T(8,128)(2,1)} %maximum_select_fusion.3), channel_id=1, source_target_pairs={{0,128},{8,136},{16,144},{24,152},{32,160},{40,168},{48,176},{56,1... | collective-permute-start | bytes 786440 | tf_op jit(solution)/shard_map/ppermute | solution.py:16
  166.0 1.5 collective-permute-start.23
  176.6 1.6 fusion.114
  180.7 1.3 add.555
  182.1 1.4 add.556
  188.6 1.5 fusion.113
  191.4 1.7 add_add_fusion
  193.1 1.6 div.199
  199.1 21.5 %psum.7 = f32[512]{0:T(512)S(1)} all-reduce(f32[512]{0:T(512)S(1)} %reduce_sum.282), channel_id=1, replica_groups=mesh['seq'=32,'head'=8] {'head'}, use_global_device_ids=true, to_apply=%region_28.29 | all-reduce | flops 512 | bytes 4096 | tf_op jit(solution)/shard_map/psum | solution.py:209
  (299 shorter events, 82.2 us)
Async XLA Ops:
  5.7 14.2 %copy-start = (bf16[512,512]{1,0:T(8,128)(2,1)S(1)}, bf16[512,512]{1,0:T(8,128)(2,1)}, u32[]{:S(2)}) copy-start(bf16[512,512]{1,0:T(8,128)(2,1)} %param.5) | copy-start | bytes 1572868
  8.4 77.0 %collective-permute-start.6 = (bf16[2,64,4,128]{3,1,2,0:T(8,128)(2,1)}, bf16[2,64,4,128]{3,1,2,0:T(8,128)(2,1)}, u32[]{:S(2)}, u32[]{:S(2)}) collective-permute-start(bf16[2,64,4,128]{3,1,2,0:T(8,128)(2,1)} %pad_maximum_fusion.14), channel_id=1, source_target_pairs={{0,8},{8,0},{16,24},{24,16},{32,40},{40,32},{48,56},{56,48},{64,72... | collective-permute-start | bytes 393224 | tf_op jit(solution)/shard_map/ppermute | solution.py:33
  11.6 58.0 %collective-permute-start.9 = (bf16[2,32,4,128]{3,1,2,0:T(8,128)(2,1)}, bf16[2,32,4,128]{3,1,2,0:T(8,128)(2,1)}, u32[]{:S(2)}, u32[]{:S(2)}) collective-permute-start(bf16[2,32,4,128]{3,1,2,0:T(8,128)(2,1)} %pad_maximum_fusion.15), channel_id=1, source_target_pairs={{0,8},{8,0},{16,24},{24,16},{32,40},{40,32},{48,56},{56,48},{64,72... | collective-permute-start | bytes 196616 | tf_op jit(solution)/shard_map/ppermute | solution.py:33
  12.3 50.4 %collective-permute-start.13 = (bf16[2,16,4,128]{3,1,2,0:T(8,128)(2,1)}, bf16[2,16,4,128]{3,1,2,0:T(8,128)(2,1)}, u32[]{:S(2)}, u32[]{:S(2)}) collective-permute-start(bf16[2,16,4,128]{3,1,2,0:T(8,128)(2,1)} %pad_maximum_fusion.16), channel_id=1, source_target_pairs={{0,8},{8,0},{16,24},{24,16},{32,40},{40,32},{48,56},{56,48},{64,72... | collective-permute-start | bytes 98312 | tf_op jit(solution)/shard_map/ppermute | solution.py:33
  14.4 44.4 %collective-permute-start.18 = (bf16[2,8,4,128]{3,1,2,0:T(8,128)(2,1)}, bf16[2,8,4,128]{3,1,2,0:T(8,128)(2,1)}, u32[]{:S(2)}, u32[]{:S(2)}) collective-permute-start(bf16[2,8,4,128]{3,1,2,0:T(8,128)(2,1)} %pad_maximum_fusion.17), channel_id=1, source_target_pairs={{0,8},{8,0},{16,24},{24,16},{32,40},{40,32},{48,56},{56,48},{64,72... | collective-permute-start | bytes 49160 | tf_op jit(solution)/shard_map/ppermute | solution.py:33
  15.3 100.2 %collective-permute-start.4 = (bf16[2,128,4,128]{3,1,2,0:T(8,128)(2,1)}, bf16[2,128,4,128]{3,1,2,0:T(8,128)(2,1)}, u32[]{:S(2)}, u32[]{:S(2)}) collective-permute-start(bf16[2,128,4,128]{3,1,2,0:T(8,128)(2,1)} %pad_maximum_fusion.13), channel_id=1, source_target_pairs={{0,8},{8,16},{16,24},{24,32},{32,40},{40,48},{48,56},{56,64},{64,7... | collective-permute-start | bytes 786440 | tf_op jit(solution)/shard_map/ppermute | solution.py:26
  40.8 13.3 %copy-start.36 = (s32[128]{0:T(128)S(1)}, s32[128]{0:T(128)}, u32[]{:S(2)}) copy-start(s32[128]{0:T(128)} %and_select_fusion.4) | copy-start | bytes 1540
  40.8 13.3 %copy-start.56 = (s32[8]{0:T(128)S(1)}, s32[8]{0:T(128)}, u32[]{:S(2)}) copy-start(s32[8]{0:T(128)} %and_select_fusion) | copy-start | bytes 100
  54.1 14.2 %copy-start.25 = (bf16[2,128,4,128]{1,3,2,0:T(8,128)(2,1)S(1)}, bf16[2,128,4,128]{1,3,2,0:T(8,128)(2,1)}, u32[]{:S(2)}) copy-start(bf16[2,128,4,128]{1,3,2,0:T(8,128)(2,1)} %get-tuple-element.8) | copy-start | bytes 786436
  54.1 19.0 %copy-start.19 = (bf16[1,32,4,128]{3,1,2,0:T(8,128)(2,1)S(1)}, bf16[1,32,4,128]{3,1,2,0:T(8,128)(2,1)}, u32[]{:S(2)}) copy-start(bf16[1,32,4,128]{3,1,2,0:T(8,128)(2,1)} %copy-done.18) | copy-start | bytes 98308
  54.1 19.0 %copy-start.21 = (bf16[1,32,4,128]{3,1,2,0:T(8,128)(2,1)S(1)}, bf16[1,32,4,128]{3,1,2,0:T(8,128)(2,1)}, u32[]{:S(2)}) copy-start(bf16[1,32,4,128]{3,1,2,0:T(8,128)(2,1)} %copy-done.20) | copy-start | bytes 98308
  58.8 46.5 %collective-permute-start = (bf16[2,128,4,128]{1,3,2,0:T(8,128)(2,1)}, bf16[2,128,4,128]{1,3,2,0:T(8,128)(2,1)S(1)}, u32[]{:S(2)}, u32[]{:S(2)}) collective-permute-start(bf16[2,128,4,128]{1,3,2,0:T(8,128)(2,1)} %get-tuple-element.7), channel_id=1, source_target_pairs={{0,8},{8,16},{16,24},{24,32},{32,40},{40,48},{48,56},{56,64},{64,7... | collective-permute-start | bytes 786440 | tf_op jit(solution)/shard_map/ppermute | solution.py:26
  62.7 5.6 %collective-permute-start.19 = (bf16[2,16,4,128]{3,1,2,0:T(8,128)(2,1)S(1)}, bf16[2,16,4,128]{3,1,2,0:T(8,128)(2,1)S(1)}, u32[]{:S(2)}, u32[]{:S(2)}) collective-permute-start(bf16[2,16,4,128]{3,1,2,0:T(8,128)(2,1)S(1)} %maximum_select_fusion.9), channel_id=1, source_target_pairs={{0,16},{8,24},{16,0},{24,8},{32,48},{40,56},{48,32},{56,40},{64,80... | collective-permute-start | bytes 98312 | tf_op jit(solution)/shard_map/ppermute | solution.py:33
  68.3 38.3 %collective-permute-start.1 = (bf16[2,128,4,128]{1,3,2,0:T(8,128)(2,1)S(1)}, bf16[2,128,4,128]{1,3,2,0:T(8,128)(2,1)S(1)}, u32[]{:S(2)}, u32[]{:S(2)}) collective-permute-start(bf16[2,128,4,128]{1,3,2,0:T(8,128)(2,1)S(1)} %copy-done.25), channel_id=1, source_target_pairs={{8,0},{16,8},{24,16},{32,24},{40,32},{48,40},{56,48},{64,56},{72,6... | collective-permute-start | bytes 786440 | tf_op jit(solution)/shard_map/ppermute | solution.py:27
  69.6 8.0 %collective-permute-start.14 = (bf16[2,32,4,128]{3,1,2,0:T(8,128)(2,1)S(1)}, bf16[2,32,4,128]{3,1,2,0:T(8,128)(2,1)S(1)}, u32[]{:S(2)}, u32[]{:S(2)}) collective-permute-start(bf16[2,32,4,128]{3,1,2,0:T(8,128)(2,1)S(1)} %maximum_select_fusion.7), channel_id=1, source_target_pairs={{0,16},{8,24},{16,0},{24,8},{32,48},{40,56},{48,32},{56,40},{64,80... | collective-permute-start | bytes 196616 | tf_op jit(solution)/shard_map/ppermute | solution.py:33
  77.6 7.7 %collective-permute-start.20 = (bf16[2,32,4,128]{3,1,2,0:T(8,128)(2,1)S(1)}, bf16[2,32,4,128]{3,1,2,0:T(8,128)(2,1)S(1)}, u32[]{:S(2)}, u32[]{:S(2)}) collective-permute-start(bf16[2,32,4,128]{3,1,2,0:T(8,128)(2,1)S(1)} %maximum_select_fusion.8), channel_id=1, source_target_pairs={{0,32},{8,40},{16,48},{24,56},{32,0},{40,8},{48,16},{56,24},{64,96... | collective-permute-start | bytes 196616 | tf_op jit(solution)/shard_map/ppermute | solution.py:33
  85.3 6.6 %collective-permute-start.10 = (bf16[2,64,4,128]{3,1,2,0:T(8,128)(2,1)S(1)}, bf16[2,64,4,128]{3,1,2,0:T(8,128)(2,1)S(1)}, u32[]{:S(2)}, u32[]{:S(2)}) collective-permute-start(bf16[2,64,4,128]{3,1,2,0:T(8,128)(2,1)S(1)} %maximum_select_fusion.4), channel_id=1, source_target_pairs={{0,16},{8,24},{16,0},{24,8},{32,48},{40,56},{48,32},{56,40},{64,80... | collective-permute-start | bytes 393224 | tf_op jit(solution)/shard_map/ppermute | solution.py:33
  85.4 12.4 %collective-permute-start.15 = (bf16[2,64,4,128]{3,1,2,0:T(8,128)(2,1)S(1)}, bf16[2,64,4,128]{3,1,2,0:T(8,128)(2,1)S(1)}, u32[]{:S(2)}, u32[]{:S(2)}) collective-permute-start(bf16[2,64,4,128]{3,1,2,0:T(8,128)(2,1)S(1)} %maximum_select_fusion.5), channel_id=1, source_target_pairs={{0,32},{8,40},{16,48},{24,56},{32,0},{40,8},{48,16},{56,24},{64,96... | collective-permute-start | bytes 393224 | tf_op jit(solution)/shard_map/ppermute | solution.py:33
  91.9 7.9 %collective-permute-start.21 = (bf16[2,64,4,128]{3,1,2,0:T(8,128)(2,1)S(1)}, bf16[2,64,4,128]{3,1,2,0:T(8,128)(2,1)S(1)}, u32[]{:S(2)}, u32[]{:S(2)}) collective-permute-start(bf16[2,64,4,128]{3,1,2,0:T(8,128)(2,1)S(1)} %maximum_select_fusion.6), channel_id=1, source_target_pairs={{0,64},{8,72},{16,80},{24,88},{32,96},{40,104},{48,112},{56,120},{... | collective-permute-start | bytes 393224 | tf_op jit(solution)/shard_map/ppermute | solution.py:33
  97.8 19.1 %collective-permute-start.5 = (bf16[2,128,4,128]{3,1,2,0:T(8,128)(2,1)}, bf16[2,128,4,128]{3,1,2,0:T(8,128)(2,1)}, u32[]{:S(2)}, u32[]{:S(2)}) collective-permute-start(bf16[2,128,4,128]{3,1,2,0:T(8,128)(2,1)} %pad_maximum_fusion.13), channel_id=1, source_target_pairs={{8,0},{16,8},{24,16},{32,24},{40,32},{48,40},{56,48},{64,56},{72,6... | collective-permute-start | bytes 786440 | tf_op jit(solution)/shard_map/ppermute | solution.py:27
  99.8 33.5 %collective-permute-start.2 = (bf16[2,128,4,128]{3,2,1,0:T(4,128)(2,1)}, bf16[2,128,4,128]{3,2,1,0:T(4,128)(2,1)}, u32[]{:S(2)}, u32[]{:S(2)}) collective-permute-start(bf16[2,128,4,128]{3,2,1,0:T(4,128)(2,1)} %get-tuple-element.12), channel_id=1, source_target_pairs={{0,8},{8,16},{16,24},{24,32},{32,40},{40,48},{48,56},{56,64},{64,7... | collective-permute-start | bytes 786440 | tf_op jit(solution)/shard_map/ppermute | solution.py:26
  105.3 29.3 %collective-permute-start.3 = (bf16[2,128,4,128]{3,2,1,0:T(4,128)(2,1)}, bf16[2,128,4,128]{3,2,1,0:T(4,128)(2,1)}, u32[]{:S(2)}, u32[]{:S(2)}) collective-permute-start(bf16[2,128,4,128]{3,2,1,0:T(4,128)(2,1)} %get-tuple-element.11), channel_id=1, source_target_pairs={{8,0},{16,8},{24,16},{32,24},{40,32},{48,40},{56,48},{64,56},{72,6... | collective-permute-start | bytes 786440 | tf_op jit(solution)/shard_map/ppermute | solution.py:27
  106.6 46.1 %collective-permute-start.7 = (bf16[2,128,4,128]{3,1,2,0:T(8,128)(2,1)}, bf16[2,128,4,128]{3,1,2,0:T(8,128)(2,1)}, u32[]{:S(2)}, u32[]{:S(2)}) collective-permute-start(bf16[2,128,4,128]{3,1,2,0:T(8,128)(2,1)} %maximum_select_fusion), channel_id=1, source_target_pairs={{0,16},{8,24},{16,32},{24,40},{32,48},{40,56},{48,64},{56,72},{64,... | collective-permute-start | bytes 786440 | tf_op jit(solution)/shard_map/ppermute | solution.py:16
  114.9 34.7 %copy-start.43 = (f32[4,4,128]{2,1,0:T(4,128)}, f32[4,4,128]{2,1,0:T(4,128)S(1)}, u32[]{:S(2)}) copy-start(f32[4,4,128]{2,1,0:T(4,128)S(1)} %get-tuple-element.39) | copy-start | bytes 24580
  115.6 39.4 %collective-permute-start.8 = (bf16[2,128,4,128]{3,1,2,0:T(8,128)(2,1)}, bf16[2,128,4,128]{3,1,2,0:T(8,128)(2,1)}, u32[]{:S(2)}, u32[]{:S(2)}) collective-permute-start(bf16[2,128,4,128]{3,1,2,0:T(8,128)(2,1)} %maximum_select_fusion), channel_id=1, source_target_pairs={{16,0},{24,8},{32,16},{40,24},{48,32},{56,40},{64,48},{72,56},{80,... | collective-permute-start | bytes 786440 | tf_op jit(solution)/shard_map/ppermute | solution.py:16
  116.9 49.1 %collective-permute-start.11 = (bf16[2,128,4,128]{3,1,2,0:T(8,128)(2,1)}, bf16[2,128,4,128]{3,1,2,0:T(8,128)(2,1)}, u32[]{:S(2)}, u32[]{:S(2)}) collective-permute-start(bf16[2,128,4,128]{3,1,2,0:T(8,128)(2,1)} %maximum_select_fusion.1), channel_id=1, source_target_pairs={{0,32},{8,40},{16,48},{24,56},{32,64},{40,72},{48,80},{56,88},{64,... | collective-permute-start | bytes 786440 | tf_op jit(solution)/shard_map/ppermute | solution.py:16
  129.4 14.4 %copy-start.3 = (bf16[1,256,4,128]{3,2,1,0:T(4,128)(2,1)S(1)}, bf16[1,256,4,128]{3,2,1,0:T(4,128)(2,1)}, u32[]{:S(2)}) copy-start(bf16[1,256,4,128]{3,2,1,0:T(4,128)(2,1)} %get-tuple-element.51) | copy-start | bytes 786436
  130.3 16.6 %copy-start.35 = (pred[2,128,256]{2,1,0:T(8,128)(4,1)S(1)}, pred[2,128,256]{2,1,0:T(8,128)(4,1)}, u32[]{:S(2)}) copy-start(pred[2,128,256]{2,1,0:T(8,128)(4,1)} %pad_add_fusion.1) | copy-start | bytes 196612
  133.3 35.2 %collective-permute-start.12 = (bf16[2,128,4,128]{3,1,2,0:T(8,128)(2,1)}, bf16[2,128,4,128]{3,1,2,0:T(8,128)(2,1)}, u32[]{:S(2)}, u32[]{:S(2)}) collective-permute-start(bf16[2,128,4,128]{3,1,2,0:T(8,128)(2,1)} %maximum_select_fusion.1), channel_id=1, source_target_pairs={{32,0},{40,8},{48,16},{56,24},{64,32},{72,40},{80,48},{88,56},{96,... | collective-permute-start | bytes 786440 | tf_op jit(solution)/shard_map/ppermute | solution.py:16
  134.6 39.1 %collective-permute-start.16 = (bf16[2,128,4,128]{3,1,2,0:T(8,128)(2,1)}, bf16[2,128,4,128]{3,1,2,0:T(8,128)(2,1)}, u32[]{:S(2)}, u32[]{:S(2)}) collective-permute-start(bf16[2,128,4,128]{3,1,2,0:T(8,128)(2,1)} %maximum_select_fusion.2), channel_id=1, source_target_pairs={{0,64},{8,72},{16,80},{24,88},{32,96},{40,104},{48,112},{56,120},{... | collective-permute-start | bytes 786440 | tf_op jit(solution)/shard_map/ppermute | solution.py:16
  148.3 13.4 %copy-start.12 = (f32[64,4,128]{2,1,0:T(4,128)S(1)}, f32[64,4,128]{2,1,0:T(4,128)}, u32[]{:S(2)}) copy-start(f32[64,4,128]{2,1,0:T(4,128)} %copy-done.11) | copy-start | bytes 393220
  148.4 13.4 %copy-start.49 = (pred[64,256]{1,0:T(8,128)(4,1)S(1)}, pred[64,256]{1,0:T(8,128)(4,1)}, u32[]{:S(2)}) copy-start(pred[64,256]{1,0:T(8,128)(4,1)} %pad_add_fusion.2) | copy-start | bytes 49156
  151.6 18.6 %copy-start.23 = (f32[32,4,128]{2,1,0:T(4,128)S(1)}, f32[32,4,128]{2,1,0:T(4,128)}, u32[]{:S(2)}) copy-start(f32[32,4,128]{2,1,0:T(4,128)} %copy-done.22) | copy-start | bytes 196612
  151.6 18.6 %copy-start.51 = (pred[32,256]{1,0:T(8,128)(4,1)S(1)}, pred[32,256]{1,0:T(8,128)(4,1)}, u32[]{:S(2)}) copy-start(pred[32,256]{1,0:T(8,128)(4,1)} %pad_add_fusion.3) | copy-start | bytes 24580
  152.7 23.8 %copy-start.53 = (pred[16,256]{1,0:T(8,128)(4,1)S(1)}, pred[16,256]{1,0:T(8,128)(4,1)}, u32[]{:S(2)}) copy-start(pred[16,256]{1,0:T(8,128)(4,1)} %pad_add_fusion.4) | copy-start | bytes 12292
  152.7 22.0 %collective-permute-start.17 = (bf16[2,128,4,128]{3,1,2,0:T(8,128)(2,1)}, bf16[2,128,4,128]{3,1,2,0:T(8,128)(2,1)}, u32[]{:S(2)}, u32[]{:S(2)}) collective-permute-start(bf16[2,128,4,128]{3,1,2,0:T(8,128)(2,1)} %maximum_select_fusion.2), channel_id=1, source_target_pairs={{64,0},{72,8},{80,16},{88,24},{96,32},{104,40},{112,48},{120,56},{... | collective-permute-start | bytes 786440 | tf_op jit(solution)/shard_map/ppermute | solution.py:16
  155.0 30.8 %collective-permute-start.22 = (bf16[2,128,4,128]{3,1,2,0:T(8,128)(2,1)}, bf16[2,128,4,128]{3,1,2,0:T(8,128)(2,1)}, u32[]{:S(2)}, u32[]{:S(2)}) collective-permute-start(bf16[2,128,4,128]{3,1,2,0:T(8,128)(2,1)} %maximum_select_fusion.3), channel_id=1, source_target_pairs={{0,128},{8,136},{16,144},{24,152},{32,160},{40,168},{48,176},{56,1... | collective-permute-start | bytes 786440 | tf_op jit(solution)/shard_map/ppermute | solution.py:16
  166.0 20.9 %collective-permute-start.23 = (bf16[2,128,4,128]{3,1,2,0:T(8,128)(2,1)}, bf16[2,128,4,128]{3,1,2,0:T(8,128)(2,1)}, u32[]{:S(2)}, u32[]{:S(2)}) collective-permute-start(bf16[2,128,4,128]{3,1,2,0:T(8,128)(2,1)} %maximum_select_fusion.3), channel_id=1, source_target_pairs={{128,0},{136,8},{144,16},{152,24},{160,32},{168,40},{176,48},{184,... | collective-permute-start | bytes 786440 | tf_op jit(solution)/shard_map/ppermute | solution.py:16
  174.7 23.3 %copy-start.7 = (f32[128,4,128]{2,0,1:T(8,128)S(1)}, f32[128,4,128]{2,0,1:T(8,128)}, u32[]{:S(2)}) copy-start(f32[128,4,128]{2,0,1:T(8,128)} %copy.433) | copy-start | bytes 786436
  198.2 22.4 %copy-start.47 = (f32[8,4]{0,1:T(4,128)S(1)}, f32[8,4]{0,1:T(4,128)}, u32[]{:S(2)}) copy-start(f32[8,4]{0,1:T(4,128)} %copy-done.46) | copy-start | bytes 388
  198.2 22.6 %copy-start.38 = (f32[512,4]{0,1:T(4,128)S(1)}, f32[512,4]{0,1:T(4,128)}, u32[]{:S(2)}) copy-start(f32[512,4]{0,1:T(4,128)} %add.544) | copy-start | bytes 24580
  198.2 22.5 %copy-start.39 = (f32[512,4]{0,1:T(4,128)S(1)}, f32[512,4]{0,1:T(4,128)}, u32[]{:S(2)}) copy-start(f32[512,4]{0,1:T(4,128)} %copy.452) | copy-start | bytes 24580
  198.2 22.5 %copy-start.40 = (f32[512,4]{0,1:T(4,128)S(1)}, f32[512,4]{0,1:T(4,128)}, u32[]{:S(2)}) copy-start(f32[512,4]{0,1:T(4,128)} %add.548) | copy-start | bytes 24580
  198.3 22.5 %copy-start.41 = (f32[512,4]{0,1:T(4,128)S(1)}, f32[512,4]{0,1:T(4,128)}, u32[]{:S(2)}) copy-start(f32[512,4]{0,1:T(4,128)} %add.552) | copy-start | bytes 24580
  198.3 22.5 %copy-start.42 = (f32[512,4]{0,1:T(4,128)S(1)}, f32[512,4]{0,1:T(4,128)}, u32[]{:S(2)}) copy-start(f32[512,4]{0,1:T(4,128)} %add.556) | copy-start | bytes 24580
  198.3 22.5 %copy-start.44 = (f32[4,4,128]{2,1,0:T(4,128)S(1)}, f32[4,4,128]{2,1,0:T(4,128)}, u32[]{:S(2)}) copy-start(f32[4,4,128]{2,1,0:T(4,128)} %copy-done.43) | copy-start | bytes 24580
  198.3 23.3 %copy-start.24 = (f32[32,4,128]{2,1,0:T(4,128)S(1)}, f32[32,4,128]{2,1,0:T(4,128)}, u32[]{:S(2)}) copy-start(f32[32,4,128]{2,1,0:T(4,128)} %copy.442) | copy-start | bytes 196612
  198.8 23.0 %copy-start.30 = (f32[16,4,128]{2,1,0:T(4,128)S(1)}, f32[16,4,128]{2,1,0:T(4,128)}, u32[]{:S(2)}) copy-start(f32[16,4,128]{2,1,0:T(4,128)} %copy.446) | copy-start | bytes 98308
  (33 other events, 69.9 us)
where the time goes:
time: 227 us; the launch traced here: 224 us
  starting transfers between devices  70.4 us (31%)
  local copies, waits for them, and re-layouts  54 us (24%)
  other arithmetic  49 us (22%)
  blocking collectives  21.5 us (9%)
  matrix products  16.1 us (7%)
  waiting for transfers between devices  11.4 us (5%)
    ppermute x8, starting transfers between devices, from_behind(): return lax.ppermute(block, axis, route)  32.9 us
    ppermute x10, starting transfers between devices, from_partner(): lax.ppermute(x, axis, [(i, i ^ 1 << bit) for i in range(lax.axis_size(axi...  21.9 us
    psum x1, blocking collectives, on_device(): token_total = lax.psum(jnp.sum(scaled * scaled, axis=(1, 2)), 'head')  21.5 us
    unnamed x125, local copies, waits for them, and re-layouts  15.3 us
    ppermute x3, starting transfers between devices, extended_2(): before = lax.ppermute(last, axis, up)  11.8 us
    add x24, local copies, waits for them, and re-layouts, spread_add(): denominator.reshape(coarse_rows, repeat_factor, head_count)  11.6 us
    ppermute x10, waiting for transfers between devices, from_partner(): lax.ppermute(x, axis, [(i, i ^ 1 << bit) for i in range(lax.axis_size(axi...  11.4 us
    dot_general x7, matrix products, attend(): jnp.einsum('bqhe,bkhe->bhqk', query_tiles, key_blocks, preferred_element_...  8.32 us
  transfers between devices with their start and end apart: 24, of which 4 were waited for; matrix products, arithmetic and copies ran while one was open for 40% of the time, Pallas kernels for 0%

commit v1 on v0

v1 whole, which is shorter than its diff:
```python
import jax
import jax.numpy as jnp
from jax import lax
from jax.experimental import pallas as pl
from jax.experimental.pallas import tpu as pltpu
from jax.sharding import PartitionSpec as P

MESH = pl.DeviceIdType.MESH
BF = jnp.bfloat16
F32 = jnp.float32
EPSILON = 1e-06
E = 128
ROWS = 512
HD = 4
WIDTH = HD * E
SCALE = E ** (-0.5)
NX, NZ, NSEQ, NHEAD = 4, 8, 32, 8


def iota(shape, dim):
    return lax.broadcasted_iota(jnp.int32, shape, dim)


def pool_matrix(parts, columns):
    out = []
    for rows, shift, offset, repeat in parts:
        group = iota((rows, columns), 0) // repeat + offset
        inside = (iota((rows, columns), 1) >> shift) == group
        out.append(jnp.where(inside, 0.5**shift, 0.0))
    return jnp.concatenate(out, axis=0).astype(BF)


def dot(a, b):
    return jnp.dot(a, b, preferred_element_type=F32)


def attn(q, k, v, mask=None):
    logits = lax.dot_general(q, k, (((1,), (1,)), ((), ())), preferred_element_type=F32)
    p = jnp.exp(logits * SCALE)
    if mask is not None:
        p = p * mask
    va = jnp.concatenate([v, jnp.ones(v.shape, BF)], axis=1)
    return dot(p.astype(BF), va)


def half_mask(rows, before_on, after_on):
    qh = iota((rows, 256), 0) // 64
    col = iota((rows, 256), 1)
    kh = (col % 128) // 64
    before = jnp.where(kh <= qh, before_on, 0.0)
    after = jnp.where(kh >= qh, after_on, 0.0)
    return jnp.where(col < 128, before, after)


def split(x):
    hi = x.astype(BF).astype(F32)
    return hi, x - hi


def unit(x):
    x = x.astype(F32)
    return (x * lax.rsqrt(jnp.mean(x * x, axis=-1, keepdims=True) + EPSILON)).astype(BF)


def spread(acc, coarse, h, rows):
    base = h * 2 * rows
    for off in range(2):
        at = pl.ds(base + off, rows, stride=2)
        for t in range(2):
            acc[t, at, :] += coarse[t]


def put(acc, start, pair):
    for t in range(2):
        acc[t, pl.ds(start, pair.shape[0]), :] = pair[:, t * E : (t + 1) * E]


def kernel(
    q_ref, k_ref, v_ref, scale_ref, gain_ref, o_ref,
    qu, kv0, q1, kv1, q2, kv2, q3, kv3, small, ra, rb, rc, rd, re,
    rq3, r3, u3, w3, u_own, u_oth, w_own, w_oth, o3,
    acc0, acc1, acc2, acc3, acc4, pw, send, recv, near_recv, pw_send, pw_recv, local,
):
    d = lax.axis_index("seq")
    me = lax.axis_index("head")
    x, z = d // NZ, d % NZ
    s, r = z // 4, z % 4
    g, par = d // 2, d % 2
    left, right = (d + NSEQ - 1) % NSEQ, (d + 1) % NSEQ
    x_with = (x + 2 * s - 1 + NX) % NX
    x_back = (x - (2 * s - 1) + NX) % NX
    x_far = (x + 2) % NX
    pair_before, pair_after = (g + 15) % 16, (g + 1) % 16

    def at(row, col):
        return row * NZ + col

    bar = pltpu.get_barrier_semaphore()

    def signal(seq, head):
        pl.semaphore_signal(bar, inc=1, device_id=(seq, head), device_id_type=MESH)

    for j in range(1, 8):
        signal(at(x, (z + j) % NZ), me)
        signal(d, (me + j) % NHEAD)
    for i in range(8):
        signal(at(x_back, i), me)
    for i in range(4):
        signal(at(x_far, 4 * s + i), me)
    for i in range(2):
        signal(2 * pair_before + i, me)
        signal(2 * pair_after + i, me)

    for h in range(HD):
        c = slice(h * E, (h + 1) * E)
        qu[:, c] = unit(q_ref[:, c])
        kv0[0, 128:640, c] = unit(k_ref[:, c])
    kv0[1, 128:640, :] = v_ref[...]

    wide = pool_matrix(((128, 1, 0, 1), (64, 2, 0, 1), (32, 3, 0, 1)), 256)
    small_q = pool_matrix(((32, 4, 0, 1), (16, 5, 0, 1), (16, 6, 0, 2)), ROWS)
    small_k = pool_matrix(((32, 4, 0, 1), (16, 5, 0, 1), (16, 6, 0, 1)), ROWS)

    sq = dot(small_q, qu[...])
    sk = dot(small_k, kv0[0, 128:640, :])
    sv = dot(small_k, kv0[1, 128:640, :])
    for h in range(HD):
        c = slice(h * E, (h + 1) * E)
        small[h, 0:64] = sq[:, c].astype(BF)
        small[h, 64:96] = sk[0:32, c].astype(BF)
        small[h, 96:128] = sv[0:32, c].astype(BF)
        small[h, 128:144] = sk[32:48, c].astype(BF)
        small[h, 144:160] = sv[32:48, c].astype(BF)
        small[h, 160:176] = jnp.concatenate([sk[48:56, c], sv[48:56, c]], axis=0).astype(BF)
    for chunk in range(2):
        rows = slice(chunk * 256, chunk * 256 + 256)
        shifted = slice(chunk * 256 + 128, chunk * 256 + 384)
        for which, source in enumerate((qu[rows, :], kv0[0, shifted, :], kv0[1, shifted, :])):
            pooled = dot(wide, source).astype(BF)
            if which == 0:
                q1[chunk * 128 : chunk * 128 + 128, :] = pooled[0:128]
                q2[chunk * 64 : chunk * 64 + 64, :] = pooled[128:192]
                for i in range(2):
                    q3[i, chunk * 32 : chunk * 32 + 32, :] = pooled[192:224, i * 256 : i * 256 + 256]
            else:
                t = which - 1
                kv1[t, 128 + chunk * 128 : 256 + chunk * 128, :] = pooled[0:128]
                kv2[t, 128 + chunk * 64 : 192 + chunk * 64, :] = pooled[128:192]
                for i in range(2):
                    kv3[i, t * 64 + chunk * 32 : t * 64 + chunk * 32 + 32, :] = pooled[
                        192:224, i * 256 : i * 256 + 256
                    ]

    pl.semaphore_wait(bar, 30)
    started = []

    def start(src, dst, seq, rsem):
        copy = pltpu.make_async_remote_copy(
            src_ref=src, dst_ref=dst, send_sem=send.at[len(started)], recv_sem=rsem,
            device_id=(seq, me), device_id_type=MESH,
        )
        copy.start()
        started.append(copy)
        return copy

    own_copy = pltpu.make_async_copy(small.at[r, 32:128], ra.at[r], recv.at[0])
    own_copy.start()
    for i in range(4):
        start(small.at[i, 64:176], rc.at[r], at(x_with, 4 * s + i), recv.at[2])
        start(small.at[i, 128:176], rd.at[r], at(x_back, 4 * (1 - s) + i), recv.at[3])
        start(small.at[i, 160:176], re.at[r], at(x_far, 4 * s + i), recv.at[4])
        start(small.at[i, 0:64], rb.at[r], at(x, 4 * (1 - s) + i), recv.at[1])
    for j in range(1, 4):
        i = (r + j) % 4
        start(small.at[i, 32:128], ra.at[r], at(x, 4 * s + i), recv.at[0])
    start(q3.at[1 - par], rq3.at[par], 2 * g + 1 - par, recv.at[5])
    for i in range(2):
        start(kv3.at[i], r3.at[0, par], 2 * pair_after + i, recv.at[6])
        start(kv3.at[i], r3.at[1, par], 2 * pair_before + i, recv.at[6])
    near = []
    for t, (kv, to_right, from_left, to_left, from_right, n) in enumerate((
        (kv2, 128, 0, 192, 320, 64),
        (kv1, 256, 0, 192, 448, 64),
        (kv0, 512, 0, 128, 640, 128),
    )):
        near.append(start(kv.at[:, to_right : to_right + n], kv.at[:, from_left : from_left + n], right, near_recv.at[t]))
        near.append(start(kv.at[:, to_left : to_left + n], kv.at[:, from_right : from_right + n], left, near_recv.at[3 + t]))
    rq3[par] = q3[par]

    def own_level(h, carry):
        c = pl.ds(pl.multiple_of(h * E, E), E)
        for b in range(4):
            lo, hi = max(b - 1, 0), min(b + 2, 4)
            keys = slice(128 + lo * 128, 128 + hi * 128)
            put(acc0, h * ROWS + b * 128, attn(qu[b * 128 : b * 128 + 128, c], kv0[0, keys, c], kv0[1, keys, c]))
        return carry

    lax.fori_loop(0, HD, own_level, 0)

    for n, ref in enumerate((ra, rb, rc, rd, re)):
        pltpu.make_async_copy(ref, ref, recv.at[n]).wait()
    wrap = jnp.where(s == 1, jnp.where(x == 0, 1.0, 0.0), jnp.where(x == NX - 1, 1.0, 0.0))
    a, b, c_, d_, e_ = ra[...], rb[...], rc[...], rd[...], re[...]

    def flat(y):
        return y.reshape(y.shape[0] * y.shape[1], E)

    k4 = jnp.concatenate([flat(a[:, 32:64]), flat(c_[:, 0:32])], axis=0)
    v4 = jnp.concatenate([flat(a[:, 64:96]), flat(c_[:, 32:64])], axis=0)
    qh = iota((128, 256), 0) // 64
    col = iota((128, 256), 1)
    kh = (col % 128) // 64
    sign = 2 * s - 1
    lead = (kh - qh) * sign
    mask4 = jnp.where(
        col < 128, jnp.where(lead >= 0, 1.0, 0.0), jnp.where(lead <= 0, 1.0 - wrap, 0.0)
    )
    out4 = 16.0 * attn(flat(b[:, 0:32]), k4, v4, mask4)

    q5 = jnp.concatenate([flat(a[:, 0:16]), flat(b[:, 32:48])], axis=0)
    k5 = jnp.concatenate([flat(c_[:, 64:80]), flat(d_[:, 0:16])], axis=0)
    v5 = jnp.concatenate([flat(c_[:, 80:96]), flat(d_[:, 16:32])], axis=0)
    mask5 = jnp.where((iota((128, 128), 0) < 64) | (iota((128, 128), 1) >= 64), 1.0 - wrap, 0.0)
    out56 = 32.0 * attn(q5, k5, v5, mask5)

    q6 = jnp.concatenate([flat(a[:, 16:32]), flat(b[:, 48:64])], axis=0)
    tiles = [y.astype(F32) for y in (e_, c_[:, 96:112], d_[:, 32:48])]
    k6 = jnp.concatenate([y[i, 0:8] for y in tiles for i in range(4)], axis=0).astype(BF)
    v6 = jnp.concatenate([y[i, 8:16] for y in tiles for i in range(4)], axis=0).astype(BF)
    mask6 = jnp.where(iota((128, 96), 1) < 32, 1.0, wrap)
    out56 = out56 + 64.0 * attn(q6, k6, v6, mask6)

    lane = iota((16, E), 1)

    def den_tile(pieces):
        tile = jnp.zeros((16, E), F32)
        for n, piece in enumerate(pieces):
            hi, lo = split(piece)
            tile = jnp.where((lane >= 32 * n) & (lane < 32 * n + 16), hi, tile)
            tile = jnp.where((lane >= 32 * n + 16) & (lane < 32 * n + 32), lo, tile)
        return tile.astype(BF)

    for i in range(4):
        mine = out56[i * 16 : i * 16 + 16]
        u_own[i, 0:16] = mine[:, 0:E].astype(BF)
        u_own[i, 16:32] = den_tile([mine[:, E:]])
        other = out56[64 + i * 16 : 64 + i * 16 + 16]
        four = out4[i * 32 : i * 32 + 32]
        u_oth[i, 0:32] = four[:, 0:E].astype(BF)
        u_oth[i, 32:48] = other[:, 0:E].astype(BF)
        u_oth[i, 48:64] = den_tile([other[:, E:], four[0:16, E:], four[16:32, E:]])
    own_return = pltpu.make_async_copy(u_own.at[r], w_own.at[r], recv.at[7])
    own_return.start()
    for j in range(1, 4):
        i = (r + j) % 4
        start(u_own.at[i], w_own.at[r], at(x, 4 * s + i), recv.at[7])
    for i in range(4):
        start(u_oth.at[i], w_oth.at[r], at(x, 4 * (1 - s) + i), recv.at[8])

    pltpu.make_async_remote_copy(
        src_ref=q3.at[0], dst_ref=rq3.at[1 - par], send_sem=send.at[0], recv_sem=recv.at[5],
        device_id=(d ^ 1, me), device_id_type=MESH,
    ).wait_recv()
    pltpu.make_async_copy(r3, r3, recv.at[6]).wait()
    before_on = jnp.where(d >= 1, 1.0, 0.0)
    after_on = jnp.where(d <= NSEQ - 2, 1.0, 0.0)
    pair_before_on = jnp.where(g >= 1, 1.0, 0.0)
    pair_after_on = jnp.where(g <= 14, 1.0, 0.0)
    col192 = iota((64, 192), 1)
    for half in range(2):
        used = ((0, 0), (1, 0), (1, 1)) if half == 0 else ((0, 0), (0, 1), (1, 1))
        cut = 64 if half == 0 else 128
        mask3 = jnp.where(col192 < cut, pair_before_on, pair_after_on)
        for i in range(2):
            lanes = slice(i * E, (i + 1) * E)
            k3 = jnp.concatenate([r3[side, n, 0:64, lanes] for side, n in used], axis=0)
            v3 = jnp.concatenate([r3[side, n, 64:128, lanes] for side, n in used], axis=0)
            o3[half, i] = 8.0 * attn(rq3[half, :, lanes], k3, v3, mask3)
    lane64 = iota((64, E), 1)
    parts = []
    for i in range(2):
        put(acc3, (2 * par + i) * 64, o3[par, i])
        gone = o3[1 - par, i]
        u3[:, i * E : (i + 1) * E] = gone[:, 0:E].astype(BF)
        parts.extend(split(gone[:, E:]))
    dens = jnp.where(
        lane64 < 64, jnp.where(lane64 < 32, parts[0], parts[1]), jnp.where(lane64 < 96, parts[2], parts[3])
    )
    u3[:, 2 * E : 3 * E] = dens.astype(BF)
    back3 = start(u3, w3, 2 * g + 1 - par, recv.at[9])

    for copy in near:
        copy.wait_recv()
    fine = pool_matrix(((64, 1, 0, 1), (32, 2, 0, 1)), 128)
    coarse = pool_matrix(((32, 1, 0, 1),), 64)
    for t in range(2):
        pooled = dot(fine, kv0[t, 0:128, :]).astype(BF)
        kv1[t, 64:128, :] = pooled[0:64]
        kv2[t, 96:128, :] = pooled[64:96]
        kv2[t, 64:96, :] = dot(coarse, kv1[t, 0:64, :]).astype(BF)
        pooled = dot(fine, kv0[t, 640:768, :]).astype(BF)
        kv1[t, 384:448, :] = pooled[0:64]
        kv2[t, 256:288, :] = pooled[64:96]
        kv2[t, 288:320, :] = dot(coarse, kv1[t, 448:512, :]).astype(BF)

    def near_level(h, carry):
        c = pl.ds(pl.multiple_of(h * E, E), E)
        edges = (
            before_on * attn(qu[0:128, c], kv0[0, 0:128, c], kv0[1, 0:128, c]),
            after_on * attn(qu[384:512, c], kv0[0, 640:768, c], kv0[1, 640:768, c]),
        )
        for n, edge in enumerate(edges):
            for t in range(2):
                acc0[t, pl.ds(h * ROWS + 384 * n, 128), :] += edge[:, t * E : (t + 1) * E]
        for b in range(2):
            mask = half_mask(128, before_on if b == 0 else 1.0, after_on if b == 1 else 1.0)
            k = jnp.concatenate(
                [kv1[0, b * 128 : b * 128 + 128, c], kv1[0, 256 + b * 128 : 384 + b * 128, c]], axis=0
            )
            v = jnp.concatenate(
                [kv1[1, b * 128 : b * 128 + 128, c], kv1[1, 256 + b * 128 : 384 + b * 128, c]], axis=0
            )
            put(acc1, h * 256 + b * 128, 2.0 * attn(q1[b * 128 : b * 128 + 128, c], k, v, mask))
        k = jnp.concatenate([kv2[0, 0:128, c], kv2[0, 256:384, c]], axis=0)
        v = jnp.concatenate([kv2[1, 0:128, c], kv2[1, 256:384, c]], axis=0)
        mask = half_mask(128, before_on, after_on)
        put(acc2, h * 128, 4.0 * attn(q2[:, c], k, v, mask))
        return carry

    lax.fori_loop(0, HD, near_level, 0)

    pltpu.make_async_copy(w_own, w_own, recv.at[7]).wait()
    pltpu.make_async_copy(w_oth, w_oth, recv.at[8]).wait()
    back3.wait_recv()

    def den_of(tile, lo, hi, rows):
        return jnp.broadcast_to(tile[:, lo : lo + 1] + tile[:, hi : hi + 1], (rows, E))

    d3 = w3[:, 2 * E : 3 * E].astype(F32)
    for i in range(2):
        here = pl.ds((2 * (1 - par) + i) * 64, 64)
        acc3[0, here, :] = w3[:, i * E : (i + 1) * E].astype(F32)
        acc3[1, here, :] = den_of(d3, 64 * i, 64 * i + 32, 64)
    for h in range(HD):
        own, oth = w_own[h].astype(F32), w_oth[h].astype(F32)
        num = own[0:16] + oth[32:48]
        dt = oth[48:64]
        den = den_of(own[16:32], 0, 16, 16) + den_of(dt, 0, 16, 16)
        acc4[0, h * 32 : h * 32 + 32, :] = oth[0:32]
        acc4[1, h * 32 : h * 32 + 16, :] = den_of(dt, 32, 48, 16)
        acc4[1, h * 32 + 16 : h * 32 + 32, :] = den_of(dt, 64, 80, 16)
        spread(acc4, (num, den), h, 16)
        for acc, finer, n in ((acc4, acc3, 32), (acc3, acc2, 64), (acc2, acc1, 128), (acc1, acc0, 256)):
            spread(finer, tuple(acc[t, h * n : h * n + n, :] for t in range(2)), h, n)

    squares = jnp.zeros((ROWS, E), F32)
    for h in range(HD):
        rows = slice(h * ROWS, (h + 1) * ROWS)
        scaled = acc0[0, rows, :] / acc0[1, rows, :] * scale_ref[h]
        acc0[0, rows, :] = scaled
        squares = squares + scaled * scaled
    for n in range(4):
        turned = squares[n * 128 : n * 128 + 128].T
        pw[me, :, n * 128 : n * 128 + 128] = jnp.sum(turned, axis=0, keepdims=True)
    power = []
    for j in range(1, 8):
        copy = pltpu.make_async_remote_copy(
            src_ref=pw.at[me], dst_ref=pw.at[me], send_sem=pw_send.at[j], recv_sem=pw_recv.at[me],
            device_id=(d, (me + j) % NHEAD), device_id_type=MESH,
        )
        copy.start()
        power.append(copy)
    for j in range(1, 8):
        peer = (me + j) % NHEAD
        pltpu.make_async_remote_copy(
            src_ref=pw.at[peer], dst_ref=pw.at[peer], send_sem=pw_send.at[j], recv_sem=pw_recv.at[peer],
            device_id=(d, peer), device_id_type=MESH,
        ).wait_recv()
    total = jnp.sum(pw[...], axis=0)
    factor = lax.rsqrt(total / (NHEAD * WIDTH) + EPSILON)
    for n in range(4):
        column = jnp.broadcast_to(factor[:, n * 128 : n * 128 + 128], (128, 128)).T
        for h in range(HD):
            c = slice(h * E, (h + 1) * E)
            scaled = acc0[0, h * ROWS + n * 128 : h * ROWS + n * 128 + 128, :]
            o_ref[n * 128 : n * 128 + 128, c] = (scaled * column * gain_ref[:, c]).astype(BF)
    for copy in started:
        copy.wait_send()
    for copy in power:
        copy.wait_send()


def on_device(queries, key_inputs, value_inputs, head_scale, out_gain):
    vmem = pl.BlockSpec(memory_space=pltpu.VMEM)
    return pl.pallas_call(
        kernel,
        out_shape=jax.ShapeDtypeStruct((ROWS, WIDTH), BF),
        in_specs=[vmem, vmem, vmem, pl.BlockSpec(memory_space=pltpu.SMEM), vmem],
        out_specs=vmem,
        scratch_shapes=[
            pltpu.VMEM((512, WIDTH), BF),
            pltpu.VMEM((2, 768, WIDTH), BF),
            pltpu.VMEM((256, WIDTH), BF),
            pltpu.VMEM((2, 512, WIDTH), BF),
            pltpu.VMEM((128, WIDTH), BF),
            pltpu.VMEM((2, 384, WIDTH), BF),
            pltpu.VMEM((2, 64, 256), BF),
            pltpu.VMEM((2, 128, 256), BF),
            pltpu.VMEM((4, 176, E), BF),
            pltpu.VMEM((4, 96, E), BF),
            pltpu.VMEM((4, 64, E), BF),
            pltpu.VMEM((4, 112, E), BF),
            pltpu.VMEM((4, 48, E), BF),
            pltpu.VMEM((4, 16, E), BF),
            pltpu.VMEM((2, 64, 256), BF),
            pltpu.VMEM((2, 2, 128, 256), BF),
            pltpu.VMEM((64, 384), BF),
            pltpu.VMEM((64, 384), BF),
            pltpu.VMEM((4, 32, E), BF),
            pltpu.VMEM((4, 64, E), BF),
            pltpu.VMEM((4, 32, E), BF),
            pltpu.VMEM((4, 64, E), BF),
            pltpu.VMEM((2, 2, 64, 256), F32),
            pltpu.VMEM((2, HD * 512, E), F32),
            pltpu.VMEM((2, HD * 256, E), F32),
            pltpu.VMEM((2, HD * 128, E), F32),
            pltpu.VMEM((2, HD * 64, E), F32),
            pltpu.VMEM((2, HD * 32, E), F32),
            pltpu.VMEM((NHEAD, 1, ROWS), F32),
            pltpu.SemaphoreType.DMA((48,)),
            pltpu.SemaphoreType.DMA((10,)),
            pltpu.SemaphoreType.DMA((6,)),
            pltpu.SemaphoreType.DMA((8,)),
            pltpu.SemaphoreType.DMA((8,)),
            pltpu.SemaphoreType.DMA,
        ],
        compiler_params=pltpu.CompilerParams(
            collective_id=0, has_side_effects=True, vmem_limit_bytes=48 * 2**20
        ),
    )(queries, key_inputs, value_inputs, head_scale, out_gain.reshape(1, WIDTH))


def solution(mesh):
    placed = (P("seq", "head"), P("seq", "head"), P("seq", "head"), P("head"), P("head"))
    return jax.shard_map(
        on_device, mesh=mesh, in_specs=placed, out_specs=P("seq", "head"), check_vma=False
    )
```

time: 227 us -> 53 us (0.23); the launches traced: 224 us -> 52.7 us
  starting transfers between devices: 70.4 us -> 0 us
  other arithmetic: 49 us -> 0 us
  local copies, waits for them, and re-layouts: 54 us -> 5.25 us
  Pallas kernels: 0 us -> 47.5 us
  blocking collectives: 21.5 us -> 0 us
  matrix products: 16.1 us -> 0 us
  waiting for transfers between devices: 11.4 us -> 0 us
    ppermute x24 -> x0, starting transfers between devices: 70.4 us -> none  [the longest x8 32.9 us: from_behind(): return lax.ppermute(block, axis, route)]
    pallas_call x0 -> x1, Pallas kernels: none -> 47.5 us  [on_device(): pl.pallas_call(kernel, out_shape=jax.ShapeDtypeStruct((ROWS, WIDTH), BF),...]
    psum x1 -> x0, blocking collectives: 21.5 us -> none  [on_device(): token_total = lax.psum(jnp.sum(scaled * scaled, axis=(1, 2)), 'head')]
    add x41 -> x0, local copies, waits for them, and re-layouts: 16.8 us -> none  [the longest x24 11.6 us: spread_add(): denominator.reshape(coarse_rows, repeat_factor, head_count)]
    dot_general x14 -> x0, matrix products: 16.1 us -> none  [the longest x7 8.32 us: attend(): jnp.einsum('bqhe,bkhe->bhqk', query_tiles, key_blocks, preferred_element_...]
    ppermute x24 -> x0, waiting for transfers between devices: 11.4 us -> none  [the longest x10 11.4 us: from_partner(): lax.ppermute(x, axis, [(i, i ^ 1 << bit) for i in range(lax.axis_size(axi...]
    unnamed x125 -> x11, local copies, waits for them, and re-layouts: 15.3 us -> 5.25 us
    select_n x15 -> x0, other arithmetic: 9.64 us -> none  [the longest x10 6.88 us: on_device(): jnp.where(lower_half, jnp.concatenate([gathered_block, partner], axis=1),...]
  transfers between devices with their start and end apart: 24 -> 0, of which waited for: 4 -> 0; matrix products, arithmetic and copies ran while one was open for 40% -> 0% of each run, Pallas kernels for 0% -> 0%
where the time goes in v1:
time: 53 us; the launch traced here: 52.7 us
  Pallas kernels  47.5 us (90%)
  local copies, waits for them, and re-layouts  5.25 us (10%)
    pallas_call x1, Pallas kernels, on_device(): pl.pallas_call(kernel, out_shape=jax.ShapeDtypeStruct((ROWS, WIDTH), BF),...  47.5 us
    unnamed x11, local copies, waits for them, and re-layouts  5.25 us

profile of v1, /device:TPU:1, one launch (start us, length us, event | category | flops | bytes accessed | tf_op | source)
XLA Modules:
  0.0 52.7 jit_solution(14008646328734463469)
XLA Ops:
  0.0 0.0 copy-start.4
  0.0 0.7 %copy-done.4 = f32[4]{0:T(128)S(1)} copy-done((f32[4]{0:T(128)S(1)}, f32[4]{0:T(128)}, u32[]{:S(2)}) %copy-start.4) | copy-done | bytes 40
  0.7 0.0 copy-start
  0.7 1.0 %copy-done = bf16[512,512]{1,0:T(8,128)(2,1)S(1)} copy-done((bf16[512,512]{1,0:T(8,128)(2,1)S(1)}, bf16[512,512]{1,0:T(8,128)(2,1)}, u32[]{:S(2)}) %copy-start) | copy-done | bytes 524312
  1.7 0.0 copy-start.1
  1.7 1.0 %copy-done.1 = bf16[512,512]{1,0:T(8,128)(2,1)S(1)} copy-done((bf16[512,512]{1,0:T(8,128)(2,1)S(1)}, bf16[512,512]{1,0:T(8,128)(2,1)}, u32[]{:S(2)}) %copy-start.1) | copy-done | bytes 524312
  2.7 0.0 copy-start.2
  2.7 1.0 %copy-done.2 = bf16[512,512]{1,0:T(8,128)(2,1)S(1)} copy-done((bf16[512,512]{1,0:T(8,128)(2,1)S(1)}, bf16[512,512]{1,0:T(8,128)(2,1)}, u32[]{:S(2)}) %copy-start.2) | copy-done | bytes 524312
  3.8 0.0 copy-start.3
  3.8 0.7 %copy-done.3 = f32[512]{0:T(512)S(1)} copy-done((f32[512]{0:T(512)S(1)}, f32[512]{0:T(512)}, u32[]{:S(2)}) %copy-start.3) | copy-done | bytes 2072
  4.5 47.5 %shard_map.55 = bf16[512,512]{1,0:T(8,128)(2,1)S(1)} custom-call(bf16[512,512]{1,0:T(8,128)(2,1)S(1)} %copy-done, bf16[512,512]{1,0:T(8,128)(2,1)S(1)} %copy-done.1, bf16[512,512]{1,0:T(8,128)(2,1)S(1)} %copy-done.2, f32[4]{0:T(128)S(1)} %copy-done.4, f32[1,512]{1,0:T(1,128)S(1)} %bitcast.1), custom_call_target="tpu_custom_call" | custom-call | tf_op jit(solution)/shard_map/pallas_call | solution.py:395
  51.9 0.8 %copy.7 = bf16[512,512]{1,0:T(8,128)(2,1)} copy(bf16[512,512]{1,0:T(8,128)(2,1)S(1)} %shard_map.55) | data formatting | bytes 1048576
Async XLA Ops:
  0.0 0.7 %copy-start.4 = (f32[4]{0:T(128)S(1)}, f32[4]{0:T(128)}, u32[]{:S(2)}) copy-start(f32[4]{0:T(128)} %scale_ref.1) | copy-start | bytes 52
  0.7 1.0 %copy-start = (bf16[512,512]{1,0:T(8,128)(2,1)S(1)}, bf16[512,512]{1,0:T(8,128)(2,1)}, u32[]{:S(2)}) copy-start(bf16[512,512]{1,0:T(8,128)(2,1)} %q_ref.1) | copy-start | bytes 1572868
  1.7 1.0 %copy-start.1 = (bf16[512,512]{1,0:T(8,128)(2,1)S(1)}, bf16[512,512]{1,0:T(8,128)(2,1)}, u32[]{:S(2)}) copy-start(bf16[512,512]{1,0:T(8,128)(2,1)} %k_ref.1) | copy-start | bytes 1572868
  2.7 1.0 %copy-start.2 = (bf16[512,512]{1,0:T(8,128)(2,1)S(1)}, bf16[512,512]{1,0:T(8,128)(2,1)}, u32[]{:S(2)}) copy-start(bf16[512,512]{1,0:T(8,128)(2,1)} %v_ref.1) | copy-start | bytes 1572868
  3.8 0.7 %copy-start.3 = (f32[512]{0:T(512)S(1)}, f32[512]{0:T(512)}, u32[]{:S(2)}) copy-start(f32[512]{0:T(512)} %param.9) | copy-start | bytes 6148

commit v2 on v1

--- a/solution.py
+++ b/solution.py
@@ -76,10 +76,10 @@
 
 
 def kernel(
-    q_ref, k_ref, v_ref, scale_ref, gain_ref, o_ref,
-    qu, kv0, q1, kv1, q2, kv2, q3, kv3, small, ra, rb, rc, rd, re,
+    q_hbm, k_hbm, v_hbm, scale_hbm, gain_hbm, o_ref,
+    q_ref, k_ref, scale_ref, gain_ref, qu, kv0, q1, kv1, q2, kv2, q3, kv3, small, ra, rb, rc, rd, re,
     rq3, r3, u3, w3, u_own, u_oth, w_own, w_oth, o3,
-    acc0, acc1, acc2, acc3, acc4, pw, send, recv, near_recv, pw_send, pw_recv, local,
+    acc0, acc1, acc2, acc3, acc4, pw, send, recv, near_recv, pw_send, pw_recv, load,
 ):
     d = lax.axis_index("seq")
     me = lax.axis_index("head")
@@ -95,6 +95,15 @@
     def at(row, col):
         return row * NZ + col
 
+    loads = [
+        pltpu.make_async_copy(src, dst, load.at[n])
+        for n, (src, dst) in enumerate((
+            (k_hbm, k_ref), (v_hbm, kv0.at[1, 128:640]), (q_hbm, q_ref), (scale_hbm, scale_ref), (gain_hbm, gain_ref)
+        ))
+    ]
+    for copy in loads:
+        copy.start()
+
     bar = pltpu.get_barrier_semaphore()
 
     def signal(seq, head):
@@ -111,27 +120,30 @@
         signal(2 * pair_before + i, me)
         signal(2 * pair_after + i, me)
 
-    for h in range(HD):
-        c = slice(h * E, (h + 1) * E)
+    lanes_of = [slice(h * E, (h + 1) * E) for h in range(HD)]
+    loads[0].wait()
+    for c in lanes_of:
+        kv0[0, 128:640, c] = unit(k_ref[:, c])
+    loads[2].wait()
+    for c in lanes_of:
         qu[:, c] = unit(q_ref[:, c])
-        kv0[0, 128:640, c] = unit(k_ref[:, c])
-    kv0[1, 128:640, :] = v_ref[...]
+    for n in (1, 3, 4):
+        loads[n].wait()
 
     wide = pool_matrix(((128, 1, 0, 1), (64, 2, 0, 1), (32, 3, 0, 1)), 256)
-    small_q = pool_matrix(((32, 4, 0, 1), (16, 5, 0, 1), (16, 6, 0, 2)), ROWS)
+    small_q = pool_matrix(((32, 4, 0, 1), (16, 5, 0, 1)), ROWS)
     small_k = pool_matrix(((32, 4, 0, 1), (16, 5, 0, 1), (16, 6, 0, 1)), ROWS)
 
     sq = dot(small_q, qu[...])
     sk = dot(small_k, kv0[0, 128:640, :])
     sv = dot(small_k, kv0[1, 128:640, :])
-    for h in range(HD):
-        c = slice(h * E, (h + 1) * E)
-        small[h, 0:64] = sq[:, c].astype(BF)
-        small[h, 64:96] = sk[0:32, c].astype(BF)
-        small[h, 96:128] = sv[0:32, c].astype(BF)
-        small[h, 128:144] = sk[32:48, c].astype(BF)
-        small[h, 144:160] = sv[32:48, c].astype(BF)
-        small[h, 160:176] = jnp.concatenate([sk[48:56, c], sv[48:56, c]], axis=0).astype(BF)
+    for h, c in enumerate(lanes_of):
+        small[h, 0:48] = sq[:, c].astype(BF)
+        small[h, 48:80] = sk[0:32, c].astype(BF)
+        small[h, 80:112] = sv[0:32, c].astype(BF)
+        small[h, 112:128] = sk[32:48, c].astype(BF)
+        small[h, 128:144] = sv[32:48, c].astype(BF)
+        small[h, 144:160] = jnp.concatenate([sk[48:56, c], sv[48:56, c]], axis=0).astype(BF)
     for chunk in range(2):
         rows = slice(chunk * 256, chunk * 256 + 256)
         shifted = slice(chunk * 256 + 128, chunk * 256 + 384)
@@ -163,25 +175,25 @@
         started.append(copy)
         return copy
 
-    own_copy = pltpu.make_async_copy(small.at[r, 32:128], ra.at[r], recv.at[0])
+    own_copy = pltpu.make_async_copy(small.at[r, 32:112], ra.at[r], recv.at[0])
     own_copy.start()
     for i in range(4):
-        start(small.at[i, 64:176], rc.at[r], at(x_with, 4 * s + i), recv.at[2])
-        start(small.at[i, 128:176], rd.at[r], at(x_back, 4 * (1 - s) + i), recv.at[3])
-        start(small.at[i, 160:176], re.at[r], at(x_far, 4 * s + i), recv.at[4])
-        start(small.at[i, 0:64], rb.at[r], at(x, 4 * (1 - s) + i), recv.at[1])
+        start(small.at[i, 48:112], rc.at[r], at(x_with, 4 * s + i), recv.at[2])
+        start(small.at[i, 112:144], rd.at[r], at(x_back, 4 * (1 - s) + i), recv.at[3])
+        start(small.at[i, 144:160], re.at[r], at(x_far, 4 * s + i), recv.at[4])
+        start(small.at[i, 0:32], rb.at[r], at(x, 4 * (1 - s) + i), recv.at[1])
     for j in range(1, 4):
         i = (r + j) % 4
-        start(small.at[i, 32:128], ra.at[r], at(x, 4 * s + i), recv.at[0])
+        start(small.at[i, 32:112], ra.at[r], at(x, 4 * s + i), recv.at[0])
     start(q3.at[1 - par], rq3.at[par], 2 * g + 1 - par, recv.at[5])
     for i in range(2):
         start(kv3.at[i], r3.at[0, par], 2 * pair_after + i, recv.at[6])
         start(kv3.at[i], r3.at[1, par], 2 * pair_before + i, recv.at[6])
     near = []
     for t, (kv, to_right, from_left, to_left, from_right, n) in enumerate((
+        (kv0, 512, 0, 128, 640, 128),
+        (kv1, 256, 0, 192, 448, 64),
         (kv2, 128, 0, 192, 320, 64),
-        (kv1, 256, 0, 192, 448, 64),
-        (kv0, 512, 0, 128, 640, 128),
     )):
         near.append(start(kv.at[:, to_right : to_right + n], kv.at[:, from_left : from_left + n], right, near_recv.at[t]))
         near.append(start(kv.at[:, to_left : to_left + n], kv.at[:, from_right : from_right + n], left, near_recv.at[3 + t]))
@@ -205,8 +217,15 @@
     def flat(y):
         return y.reshape(y.shape[0] * y.shape[1], E)
 
-    k4 = jnp.concatenate([flat(a[:, 32:64]), flat(c_[:, 0:32])], axis=0)
-    v4 = jnp.concatenate([flat(a[:, 64:96]), flat(c_[:, 32:64])], axis=0)
+    kv_c = jnp.concatenate([flat(c_[:, 0:32]), flat(c_[:, 32:64])], axis=1)
+    kv_d = jnp.concatenate([flat(d_[:, 0:16]), flat(d_[:, 16:32])], axis=1)
+    k4 = jnp.concatenate([flat(a[:, 16:48]), kv_c[:, 0:E]], axis=0)
+    v4 = jnp.concatenate([flat(a[:, 48:80]), kv_c[:, E:]], axis=0)
+    q4, q5 = flat(b), flat(a[:, 0:16])
+    pooled_c = dot(pool_matrix(((64, 1, 0, 1), (32, 2, 0, 1)), 128), kv_c).astype(BF)
+    pooled_d = dot(pool_matrix(((32, 1, 0, 1),), 64), kv_d).astype(BF)
+    q_oth = dot(pool_matrix(((128, 1, 0, 2), (128, 2, 0, 4)), 128), q4).astype(BF)
+    q6 = dot(pool_matrix(((64, 1, 0, 2),), 64), q5).astype(BF)
     qh = iota((128, 256), 0) // 64
     col = iota((128, 256), 1)
     kh = (col % 128) // 64
@@ -215,20 +234,22 @@
     mask4 = jnp.where(
         col < 128, jnp.where(lead >= 0, 1.0, 0.0), jnp.where(lead <= 0, 1.0 - wrap, 0.0)
     )
-    out4 = 16.0 * attn(flat(b[:, 0:32]), k4, v4, mask4)
-
-    q5 = jnp.concatenate([flat(a[:, 0:16]), flat(b[:, 32:48])], axis=0)
-    k5 = jnp.concatenate([flat(c_[:, 64:80]), flat(d_[:, 0:16])], axis=0)
-    v5 = jnp.concatenate([flat(c_[:, 80:96]), flat(d_[:, 16:32])], axis=0)
-    mask5 = jnp.where((iota((128, 128), 0) < 64) | (iota((128, 128), 1) >= 64), 1.0 - wrap, 0.0)
-    out56 = 32.0 * attn(q5, k5, v5, mask5)
-
-    q6 = jnp.concatenate([flat(a[:, 16:32]), flat(b[:, 48:64])], axis=0)
-    tiles = [y.astype(F32) for y in (e_, c_[:, 96:112], d_[:, 32:48])]
-    k6 = jnp.concatenate([y[i, 0:8] for y in tiles for i in range(4)], axis=0).astype(BF)
-    v6 = jnp.concatenate([y[i, 8:16] for y in tiles for i in range(4)], axis=0).astype(BF)
+    k5 = jnp.concatenate([pooled_c[0:64, 0:E], kv_d[:, 0:E]], axis=0)
+    v5 = jnp.concatenate([pooled_c[0:64, E:], kv_d[:, E:]], axis=0)
+    far = e_.astype(F32)
+    k6 = jnp.concatenate(
+        [jnp.concatenate([far[i, 0:8] for i in range(4)], axis=0).astype(BF), pooled_c[64:96, 0:E], pooled_d[:, 0:E]], axis=0
+    )
+    v6 = jnp.concatenate(
+        [jnp.concatenate([far[i, 8:16] for i in range(4)], axis=0).astype(BF), pooled_c[64:96, E:], pooled_d[:, E:]], axis=0
+    )
     mask6 = jnp.where(iota((128, 96), 1) < 32, 1.0, wrap)
-    out56 = out56 + 64.0 * attn(q6, k6, v6, mask6)
+    out_own = 32.0 * (1.0 - wrap) * attn(q5, k5, v5) + 64.0 * attn(q6, k6, v6, mask6[0:64])
+    out_oth = (
+        16.0 * attn(q4, k4, v4, mask4)
+        + 32.0 * (1.0 - wrap) * attn(q_oth[0:128], kv_d[:, 0:E], kv_d[:, E:])
+        + 64.0 * attn(q_oth[128:256], k6, v6, mask6)
+    )
 
     lane = iota((16, E), 1)
 
@@ -241,14 +262,12 @@
         return tile.astype(BF)
 
     for i in range(4):
-        mine = out56[i * 16 : i * 16 + 16]
+        mine = out_own[i * 16 : i * 16 + 16]
         u_own[i, 0:16] = mine[:, 0:E].astype(BF)
         u_own[i, 16:32] = den_tile([mine[:, E:]])
-        other = out56[64 + i * 16 : 64 + i * 16 + 16]
-        four = out4[i * 32 : i * 32 + 32]
-        u_oth[i, 0:32] = four[:, 0:E].astype(BF)
-        u_oth[i, 32:48] = other[:, 0:E].astype(BF)
-        u_oth[i, 48:64] = den_tile([other[:, E:], four[0:16, E:], four[16:32, E:]])
+        other = out_oth[i * 32 : i * 32 + 32]
+        u_oth[i, 0:32] = other[:, 0:E].astype(BF)
+        u_oth[i, 32:48] = den_tile([other[0:16, E:], other[16:32, E:]])
     own_return = pltpu.make_async_copy(u_own.at[r], w_own.at[r], recv.at[7])
     own_return.start()
     for j in range(1, 4):
@@ -289,45 +308,60 @@
     u3[:, 2 * E : 3 * E] = dens.astype(BF)
     back3 = start(u3, w3, 2 * g + 1 - par, recv.at[9])
 
-    for copy in near:
-        copy.wait_recv()
     fine = pool_matrix(((64, 1, 0, 1), (32, 2, 0, 1)), 128)
     coarse = pool_matrix(((32, 1, 0, 1),), 64)
+    for copy in near[0:2]:
+        copy.wait_recv()
+
+    def edges(h, carry):
+        c = pl.ds(pl.multiple_of(h * E, E), E)
+        pair = (
+            before_on * attn(qu[0:128, c], kv0[0, 0:128, c], kv0[1, 0:128, c]),
+            after_on * attn(qu[384:512, c], kv0[0, 640:768, c], kv0[1, 640:768, c]),
+        )
+        for n, edge in enumerate(pair):
+            for t in range(2):
+                acc0[t, pl.ds(h * ROWS + 384 * n, 128), :] += edge[:, t * E : (t + 1) * E]
+        return carry
+
+    lax.fori_loop(0, HD, edges, 0)
     for t in range(2):
         pooled = dot(fine, kv0[t, 0:128, :]).astype(BF)
         kv1[t, 64:128, :] = pooled[0:64]
         kv2[t, 96:128, :] = pooled[64:96]
-        kv2[t, 64:96, :] = dot(coarse, kv1[t, 0:64, :]).astype(BF)
         pooled = dot(fine, kv0[t, 640:768, :]).astype(BF)
         kv1[t, 384:448, :] = pooled[0:64]
         kv2[t, 256:288, :] = pooled[64:96]
-        kv2[t, 288:320, :] = dot(coarse, kv1[t, 448:512, :]).astype(BF)
-
-    def near_level(h, carry):
+    for copy in near[2:4]:
+        copy.wait_recv()
+
+    def level_1(h, carry):
         c = pl.ds(pl.multiple_of(h * E, E), E)
-        edges = (
-            before_on * attn(qu[0:128, c], kv0[0, 0:128, c], kv0[1, 0:128, c]),
-            after_on * attn(qu[384:512, c], kv0[0, 640:768, c], kv0[1, 640:768, c]),
-        )
-        for n, edge in enumerate(edges):
-            for t in range(2):
-                acc0[t, pl.ds(h * ROWS + 384 * n, 128), :] += edge[:, t * E : (t + 1) * E]
         for b in range(2):
             mask = half_mask(128, before_on if b == 0 else 1.0, after_on if b == 1 else 1.0)
-            k = jnp.concatenate(
-                [kv1[0, b * 128 : b * 128 + 128, c], kv1[0, 256 + b * 128 : 384 + b * 128, c]], axis=0
-            )
-            v = jnp.concatenate(
-                [kv1[1, b * 128 : b * 128 + 128, c], kv1[1, 256 + b * 128 : 384 + b * 128, c]], axis=0
+            k, v = (
+                jnp.concatenate(
+                    [kv1[t, b * 128 : b * 128 + 128, c], kv1[t, 256 + b * 128 : 384 + b * 128, c]], axis=0
+                )
+                for t in range(2)
             )
             put(acc1, h * 256 + b * 128, 2.0 * attn(q1[b * 128 : b * 128 + 128, c], k, v, mask))
-        k = jnp.concatenate([kv2[0, 0:128, c], kv2[0, 256:384, c]], axis=0)
-        v = jnp.concatenate([kv2[1, 0:128, c], kv2[1, 256:384, c]], axis=0)
-        mask = half_mask(128, before_on, after_on)
-        put(acc2, h * 128, 4.0 * attn(q2[:, c], k, v, mask))
         return carry
 
-    lax.fori_loop(0, HD, near_level, 0)
+    lax.fori_loop(0, HD, level_1, 0)
+    for t in range(2):
+        kv2[t, 64:96, :] = dot(coarse, kv1[t, 0:64, :]).astype(BF)
+        kv2[t, 288:320, :] = dot(coarse, kv1[t, 448:512, :]).astype(BF)
+    for copy in near[4:6]:
+        copy.wait_recv()
+
+    def level_2(h, carry):
+        c = pl.ds(pl.multiple_of(h * E, E), E)
+        k, v = (jnp.concatenate([kv2[t, 0:128, c], kv2[t, 256:384, c]], axis=0) for t in range(2))
+        put(acc2, h * 128, 4.0 * attn(q2[:, c], k, v, half_mask(128, before_on, after_on)))
+        return carry
+
+    lax.fori_loop(0, HD, level_2, 0)
 
     pltpu.make_async_copy(w_own, w_own, recv.at[7]).wait()
     pltpu.make_async_copy(w_oth, w_oth, recv.at[8]).wait()
@@ -343,13 +377,10 @@
         acc3[1, here, :] = den_of(d3, 64 * i, 64 * i + 32, 64)
     for h in range(HD):
         own, oth = w_own[h].astype(F32), w_oth[h].astype(F32)
-        num = own[0:16] + oth[32:48]
-        dt = oth[48:64]
-        den = den_of(own[16:32], 0, 16, 16) + den_of(dt, 0, 16, 16)
         acc4[0, h * 32 : h * 32 + 32, :] = oth[0:32]
-        acc4[1, h * 32 : h * 32 + 16, :] = den_of(dt, 32, 48, 16)
-        acc4[1, h * 32 + 16 : h * 32 + 32, :] = den_of(dt, 64, 80, 16)
-        spread(acc4, (num, den), h, 16)
+        acc4[1, h * 32 : h * 32 + 16, :] = den_of(oth[32:48], 0, 16, 16)
+        acc4[1, h * 32 + 16 : h * 32 + 32, :] = den_of(oth[32:48], 32, 48, 16)
+        spread(acc4, (own[0:16], den_of(own[16:32], 0, 16, 16)), h, 16)
         for acc, finer, n in ((acc4, acc3, 32), (acc3, acc2, 64), (acc2, acc1, 128), (acc1, acc0, 256)):
             spread(finer, tuple(acc[t, h * n : h * n + n, :] for t in range(2)), h, n)
 
@@ -392,12 +423,17 @@
 
 def on_device(queries, key_inputs, value_inputs, head_scale, out_gain):
     vmem = pl.BlockSpec(memory_space=pltpu.VMEM)
+    hbm = pl.BlockSpec(memory_space=pltpu.HBM)
     return pl.pallas_call(
         kernel,
         out_shape=jax.ShapeDtypeStruct((ROWS, WIDTH), BF),
-        in_specs=[vmem, vmem, vmem, pl.BlockSpec(memory_space=pltpu.SMEM), vmem],
+        in_specs=[hbm] * 5,
         out_specs=vmem,
         scratch_shapes=[
+            pltpu.VMEM((512, WIDTH), BF),
+            pltpu.VMEM((512, WIDTH), BF),
+            pltpu.SMEM((HD,), F32),
+            pltpu.VMEM((1, WIDTH), F32),
             pltpu.VMEM((512, WIDTH), BF),
             pltpu.VMEM((2, 768, WIDTH), BF),
             pltpu.VMEM((256, WIDTH), BF),
@@ -406,20 +442,20 @@
             pltpu.VMEM((2, 384, WIDTH), BF),
             pltpu.VMEM((2, 64, 256), BF),
             pltpu.VMEM((2, 128, 256), BF),
-            pltpu.VMEM((4, 176, E), BF),
-            pltpu.VMEM((4, 96, E), BF),
+            pltpu.VMEM((4, 160, E), BF),
+            pltpu.VMEM((4, 80, E), BF),
+            pltpu.VMEM((4, 32, E), BF),
             pltpu.VMEM((4, 64, E), BF),
-            pltpu.VMEM((4, 112, E), BF),
-            pltpu.VMEM((4, 48, E), BF),
+            pltpu.VMEM((4, 32, E), BF),
             pltpu.VMEM((4, 16, E), BF),
             pltpu.VMEM((2, 64, 256), BF),
             pltpu.VMEM((2, 2, 128, 256), BF),
             pltpu.VMEM((64, 384), BF),
             pltpu.VMEM((64, 384), BF),
             pltpu.VMEM((4, 32, E), BF),
-            pltpu.VMEM((4, 64, E), BF),
+            pltpu.VMEM((4, 48, E), BF),
             pltpu.VMEM((4, 32, E), BF),
-            pltpu.VMEM((4, 64, E), BF),
+            pltpu.VMEM((4, 48, E), BF),
             pltpu.VMEM((2, 2, 64, 256), F32),
             pltpu.VMEM((2, HD * 512, E), F32),
             pltpu.VMEM((2, HD * 256, E), F32),
@@ -432,10 +468,10 @@
             pltpu.SemaphoreType.DMA((6,)),
             pltpu.SemaphoreType.DMA((8,)),
             pltpu.SemaphoreType.DMA((8,)),
-            pltpu.SemaphoreType.DMA,
+            pltpu.SemaphoreType.DMA((5,)),
         ],
         compiler_params=pltpu.CompilerParams(
-            collective_id=0, has_side_effects=True, vmem_limit_bytes=48 * 2**20
+            collective_id=0, has_side_effects=True, vmem_limit_bytes=60 * 2**20
         ),
     )(queries, key_inputs, value_inputs, head_scale, out_gain.reshape(1, WIDTH))
 

time: 53 us -> 46.8 us (0.88)
  local copies, waits for them, and re-layouts: 5.25 us -> 1.87 us
  Pallas kernels: 47.5 us -> 44.8 us
    unnamed x11 -> x1, local copies, waits for them, and re-layouts: 5.25 us -> 1.87 us
    pallas_call x1, Pallas kernels: 47.5 us -> 44.8 us  [on_device(): pl.pallas_call(kernel, out_shape=jax.ShapeDtypeStruct((ROWS, WIDTH), BF),...]
where the time goes in v2:
time: 46.8 us; the launch traced here: 46.7 us
  Pallas kernels  44.8 us (96%)
  local copies, waits for them, and re-layouts  1.87 us (4%)
    pallas_call x1, Pallas kernels, on_device(): pl.pallas_call(kernel, out_shape=jax.ShapeDtypeStruct((ROWS, WIDTH), BF),...  44.8 us
    unnamed x1, local copies, waits for them, and re-layouts  1.87 us

profile of v2, /device:TPU:1, one launch (start us, length us, event | category | flops | bytes accessed | tf_op | source)
XLA Modules:
  0.0 46.7 jit_solution(15686876660221485251)
XLA Ops:
  0.0 44.8 %shard_map.55 = bf16[512,512]{1,0:T(8,128)(2,1)} custom-call(bf16[512,512]{1,0:T(8,128)(2,1)} %q_hbm.1, bf16[512,512]{1,0:T(8,128)(2,1)} %k_hbm.1, bf16[512,512]{1,0:T(8,128)(2,1)} %v_hbm.1, f32[4]{0:T(128)} %scale_hbm.1, f32[1,512]{1,0:T(1,128)} %bitcast.1), custom_call_target="tpu_custom_call" | custom-call | tf_op jit(solution)/shard_map/pallas_call | solution.py:427
  44.8 1.9 %copy.7 = bf16[512,512]{1,0:T(8,128)(2,1)} copy(bf16[512,512]{1,0:T(8,128)(2,1)} %shard_map.55) | data formatting | bytes 1048576

commit v3 on v2

--- a/solution.py
+++ b/solution.py
@@ -30,6 +30,20 @@
     return jnp.concatenate(out, axis=0).astype(BF)
 
 
+def detail_matrix(rows, shift, chunk, columns):
+    k = iota((rows, columns), 0)
+    group = k % 16
+    for bit in range(3 - shift):
+        group = group * 2 + (k >> (4 + bit)) % 2
+    col = iota((rows, columns), 1) - 128 * chunk
+    sign = jnp.where((col >> (shift - 1)) % 2 == 0, 0.5**shift, -(0.5**shift))
+    return jnp.where((col >> shift) == group, sign, 0.0)
+
+
+def rebuild(coarse, detail):
+    return jnp.concatenate([coarse + detail, coarse - detail], axis=0)
+
+
 def dot(a, b):
     return jnp.dot(a, b, preferred_element_type=F32)
 
@@ -77,8 +91,8 @@
 
 def kernel(
     q_hbm, k_hbm, v_hbm, scale_hbm, gain_hbm, o_ref,
-    q_ref, k_ref, scale_ref, gain_ref, qu, kv0, q1, kv1, q2, kv2, q3, kv3, small, ra, rb, rc, rd, re,
-    rq3, r3, u3, w3, u_own, u_oth, w_own, w_oth, o3,
+    q_ref, k_ref, scale_ref, gain_ref, qu, kv0, q1, kv1, q2, kv2, q3, out_near, in_near, hop2, hop3, small, ra, rb, rc, rd, re,
+    u_own, u_oth, w_own, w_oth,
     acc0, acc1, acc2, acc3, acc4, pw, send, recv, near_recv, pw_send, pw_recv, load,
 ):
     d = lax.axis_index("seq")
@@ -90,7 +104,6 @@
     x_with = (x + 2 * s - 1 + NX) % NX
     x_back = (x - (2 * s - 1) + NX) % NX
     x_far = (x + 2) % NX
-    pair_before, pair_after = (g + 15) % 16, (g + 1) % 16
 
     def at(row, col):
         return row * NZ + col
@@ -112,13 +125,12 @@
     for j in range(1, 8):
         signal(at(x, (z + j) % NZ), me)
         signal(d, (me + j) % NHEAD)
-    for i in range(8):
-        signal(at(x_back, i), me)
     for i in range(4):
+        signal(at(x_back, 4 * s + i), me)
+        signal(at(x_with, 4 * s + i), me)
         signal(at(x_far, 4 * s + i), me)
-    for i in range(2):
-        signal(2 * pair_before + i, me)
-        signal(2 * pair_after + i, me)
+    signal(left, me)
+    signal(right, me)
 
     lanes_of = [slice(h * E, (h + 1) * E) for h in range(HD)]
     loads[0].wait()
@@ -130,7 +142,14 @@
     for n in (1, 3, 4):
         loads[n].wait()
 
-    wide = pool_matrix(((128, 1, 0, 1), (64, 2, 0, 1), (32, 3, 0, 1)), 256)
+    pools_q = pool_matrix(((128, 1, 0, 1), (64, 2, 0, 1), (32, 3, 0, 1)), 256)
+    pools_kv = jnp.concatenate(
+        [pool_matrix(((128, 1, 0, 1), (32, 3, 0, 1)), 256)]
+        + [detail_matrix(16, 3, c, 256).astype(BF) for c in range(2)]
+        + [detail_matrix(32, 2, c, 256).astype(BF) for c in range(2)],
+        axis=0,
+    )
+    finest = detail_matrix(64, 1, 0, 128).astype(BF)
     small_q = pool_matrix(((32, 4, 0, 1), (16, 5, 0, 1)), ROWS)
     small_k = pool_matrix(((32, 4, 0, 1), (16, 5, 0, 1), (16, 6, 0, 1)), ROWS)
 
@@ -144,26 +163,23 @@
         small[h, 112:128] = sk[32:48, c].astype(BF)
         small[h, 128:144] = sv[32:48, c].astype(BF)
         small[h, 144:160] = jnp.concatenate([sk[48:56, c], sv[48:56, c]], axis=0).astype(BF)
-    for chunk in range(2):
-        rows = slice(chunk * 256, chunk * 256 + 256)
-        shifted = slice(chunk * 256 + 128, chunk * 256 + 384)
-        for which, source in enumerate((qu[rows, :], kv0[0, shifted, :], kv0[1, shifted, :])):
-            pooled = dot(wide, source).astype(BF)
-            if which == 0:
-                q1[chunk * 128 : chunk * 128 + 128, :] = pooled[0:128]
-                q2[chunk * 64 : chunk * 64 + 64, :] = pooled[128:192]
-                for i in range(2):
-                    q3[i, chunk * 32 : chunk * 32 + 32, :] = pooled[192:224, i * 256 : i * 256 + 256]
-            else:
-                t = which - 1
-                kv1[t, 128 + chunk * 128 : 256 + chunk * 128, :] = pooled[0:128]
-                kv2[t, 128 + chunk * 64 : 192 + chunk * 64, :] = pooled[128:192]
-                for i in range(2):
-                    kv3[i, t * 64 + chunk * 32 : t * 64 + chunk * 32 + 32, :] = pooled[
-                        192:224, i * 256 : i * 256 + 256
-                    ]
-
-    pl.semaphore_wait(bar, 30)
+    for half in range(2):
+        rows = slice(half * 256, half * 256 + 256)
+        pooled = dot(pools_q, qu[rows, :]).astype(BF)
+        q1[half * 128 : half * 128 + 128, :] = pooled[0:128]
+        q2[half * 64 : half * 64 + 64, :] = pooled[128:192]
+        q3[half * 32 : half * 32 + 32, :] = pooled[192:224]
+        for t in range(2):
+            pooled = dot(pools_kv, kv0[t, half * 256 + 128 : half * 256 + 384, :]).astype(BF)
+            kv1[t, 128 + half * 128 : 256 + half * 128, :] = pooled[0:128]
+            out_near[t, half * 32 : half * 32 + 32, :] = pooled[128:160]
+            out_near[t, 64 + half * 32 : 96 + half * 32, :] = pooled[160:192]
+            out_near[t, 128 + half * 64 : 192 + half * 64, :] = pooled[192:256]
+            edge = 128 + half * 384
+            finest_rows = dot(finest, kv0[t, edge : edge + 128, :]).astype(BF)
+            out_near[t, 256 + half * 64 : 320 + half * 64, :] = finest_rows
+
+    pl.semaphore_wait(bar, 28)
     started = []
 
     def start(src, dst, seq, rsem):
@@ -175,29 +191,32 @@
         started.append(copy)
         return copy
 
+    near = []
+
+    def send_near(n):
+        to_left, to_right = ((0, 0), (64, 64), (128, 192), (256, 320))[n]
+        into = slice(64 * n, 64 * n + 64)
+        near.append((
+            start(out_near.at[:, to_right : to_right + 64], in_near.at[0, :, into], right, near_recv.at[n]),
+            start(out_near.at[:, to_left : to_left + 64], in_near.at[1, :, into], left, near_recv.at[4 + n]),
+        ))
+
+    def wait_both(copies):
+        for copy in copies:
+            copy.wait_recv()
+
+    send_near(0)
     own_copy = pltpu.make_async_copy(small.at[r, 32:112], ra.at[r], recv.at[0])
     own_copy.start()
     for i in range(4):
         start(small.at[i, 48:112], rc.at[r], at(x_with, 4 * s + i), recv.at[2])
-        start(small.at[i, 112:144], rd.at[r], at(x_back, 4 * (1 - s) + i), recv.at[3])
+        start(small.at[i, 112:144], rd.at[r], at(x_back, 4 * s + i), recv.at[3])
         start(small.at[i, 144:160], re.at[r], at(x_far, 4 * s + i), recv.at[4])
         start(small.at[i, 0:32], rb.at[r], at(x, 4 * (1 - s) + i), recv.at[1])
     for j in range(1, 4):
         i = (r + j) % 4
         start(small.at[i, 32:112], ra.at[r], at(x, 4 * s + i), recv.at[0])
-    start(q3.at[1 - par], rq3.at[par], 2 * g + 1 - par, recv.at[5])
-    for i in range(2):
-        start(kv3.at[i], r3.at[0, par], 2 * pair_after + i, recv.at[6])
-        start(kv3.at[i], r3.at[1, par], 2 * pair_before + i, recv.at[6])
-    near = []
-    for t, (kv, to_right, from_left, to_left, from_right, n) in enumerate((
-        (kv0, 512, 0, 128, 640, 128),
-        (kv1, 256, 0, 192, 448, 64),
-        (kv2, 128, 0, 192, 320, 64),
-    )):
-        near.append(start(kv.at[:, to_right : to_right + n], kv.at[:, from_left : from_left + n], right, near_recv.at[t]))
-        near.append(start(kv.at[:, to_left : to_left + n], kv.at[:, from_right : from_right + n], left, near_recv.at[3 + t]))
-    rq3[par] = q3[par]
+    send_near(1)
 
     def own_level(h, carry):
         c = pl.ds(pl.multiple_of(h * E, E), E)
@@ -207,11 +226,19 @@
             put(acc0, h * ROWS + b * 128, attn(qu[b * 128 : b * 128 + 128, c], kv0[0, keys, c], kv0[1, keys, c]))
         return carry
 
-    lax.fori_loop(0, HD, own_level, 0)
+    lax.fori_loop(0, 2, own_level, 0)
+    wait_both(near[0])
+    second = (
+        start(in_near.at[0, :, 0:64], hop2.at[0], right, near_recv.at[8]),
+        start(in_near.at[1, :, 0:64], hop2.at[1], left, near_recv.at[9]),
+    )
+    send_near(2)
+    lax.fori_loop(2, HD, own_level, 0)
 
     for n, ref in enumerate((ra, rb, rc, rd, re)):
         pltpu.make_async_copy(ref, ref, recv.at[n]).wait()
     wrap = jnp.where(s == 1, jnp.where(x == 0, 1.0, 0.0), jnp.where(x == NX - 1, 1.0, 0.0))
+    wrap_d = jnp.where(s == 1, jnp.where(x == NX - 1, 1.0, 0.0), jnp.where(x == 0, 1.0, 0.0))
     a, b, c_, d_, e_ = ra[...], rb[...], rc[...], rd[...], re[...]
 
     def flat(y):
@@ -243,11 +270,13 @@
     v6 = jnp.concatenate(
         [jnp.concatenate([far[i, 8:16] for i in range(4)], axis=0).astype(BF), pooled_c[64:96, E:], pooled_d[:, E:]], axis=0
     )
-    mask6 = jnp.where(iota((128, 96), 1) < 32, 1.0, wrap)
-    out_own = 32.0 * (1.0 - wrap) * attn(q5, k5, v5) + 64.0 * attn(q6, k6, v6, mask6[0:64])
+    col6 = iota((128, 96), 1)
+    mask6 = jnp.where(col6 < 32, 1.0, jnp.where(col6 < 64, wrap, wrap_d))
+    mask5 = jnp.where(iota((64, 128), 1) < 64, 1.0 - wrap, 1.0 - wrap_d)
+    out_own = 32.0 * attn(q5, k5, v5, mask5) + 64.0 * attn(q6, k6, v6, mask6[0:64])
     out_oth = (
         16.0 * attn(q4, k4, v4, mask4)
-        + 32.0 * (1.0 - wrap) * attn(q_oth[0:128], kv_d[:, 0:E], kv_d[:, E:])
+        + 32.0 * (1.0 - wrap_d) * attn(q_oth[0:128], kv_d[:, 0:E], kv_d[:, E:])
         + 64.0 * attn(q_oth[128:256], k6, v6, mask6)
     )
 
@@ -276,67 +305,50 @@
     for i in range(4):
         start(u_oth.at[i], w_oth.at[r], at(x, 4 * (1 - s) + i), recv.at[8])
 
-    pltpu.make_async_remote_copy(
-        src_ref=q3.at[0], dst_ref=rq3.at[1 - par], send_sem=send.at[0], recv_sem=recv.at[5],
-        device_id=(d ^ 1, me), device_id_type=MESH,
-    ).wait_recv()
-    pltpu.make_async_copy(r3, r3, recv.at[6]).wait()
     before_on = jnp.where(d >= 1, 1.0, 0.0)
     after_on = jnp.where(d <= NSEQ - 2, 1.0, 0.0)
     pair_before_on = jnp.where(g >= 1, 1.0, 0.0)
-    pair_after_on = jnp.where(g <= 14, 1.0, 0.0)
-    col192 = iota((64, 192), 1)
-    for half in range(2):
-        used = ((0, 0), (1, 0), (1, 1)) if half == 0 else ((0, 0), (0, 1), (1, 1))
-        cut = 64 if half == 0 else 128
-        mask3 = jnp.where(col192 < cut, pair_before_on, pair_after_on)
-        for i in range(2):
-            lanes = slice(i * E, (i + 1) * E)
-            k3 = jnp.concatenate([r3[side, n, 0:64, lanes] for side, n in used], axis=0)
-            v3 = jnp.concatenate([r3[side, n, 64:128, lanes] for side, n in used], axis=0)
-            o3[half, i] = 8.0 * attn(rq3[half, :, lanes], k3, v3, mask3)
-    lane64 = iota((64, E), 1)
-    parts = []
-    for i in range(2):
-        put(acc3, (2 * par + i) * 64, o3[par, i])
-        gone = o3[1 - par, i]
-        u3[:, i * E : (i + 1) * E] = gone[:, 0:E].astype(BF)
-        parts.extend(split(gone[:, E:]))
-    dens = jnp.where(
-        lane64 < 64, jnp.where(lane64 < 32, parts[0], parts[1]), jnp.where(lane64 < 96, parts[2], parts[3])
-    )
-    u3[:, 2 * E : 3 * E] = dens.astype(BF)
-    back3 = start(u3, w3, 2 * g + 1 - par, recv.at[9])
-
-    fine = pool_matrix(((64, 1, 0, 1), (32, 2, 0, 1)), 128)
-    coarse = pool_matrix(((32, 1, 0, 1),), 64)
-    for copy in near[0:2]:
-        copy.wait_recv()
-
-    def edges(h, carry):
-        c = pl.ds(pl.multiple_of(h * E, E), E)
-        pair = (
-            before_on * attn(qu[0:128, c], kv0[0, 0:128, c], kv0[1, 0:128, c]),
-            after_on * attn(qu[384:512, c], kv0[0, 640:768, c], kv0[1, 640:768, c]),
-        )
-        for n, edge in enumerate(pair):
-            for t in range(2):
-                acc0[t, pl.ds(h * ROWS + 384 * n, 128), :] += edge[:, t * E : (t + 1) * E]
+    pair_after_on = jnp.where(g <= NSEQ // 2 - 2, 1.0, 0.0)
+    wait_both(second)
+    third = start(hop2.at[par], hop3, 2 * g + 1 - par, near_recv.at[10])
+    send_near(3)
+
+    def head_lanes(h):
+        return pl.ds(pl.multiple_of(h * E, E), E)
+
+    def rows_of(side, t, n, chunk, rows):
+        return in_near[side, t, 64 * n + rows * chunk : 64 * n + rows * chunk + rows, :].astype(F32)
+
+    wait_both(near[1])
+    for side in range(2):
+        for t in range(2):
+            for chunk in range(4):
+                coarse = rebuild(rows_of(side, t, 0, chunk, 16), rows_of(side, t, 1, chunk, 16))
+                at_row = 256 * side + 32 * chunk
+                kv2[t, at_row : at_row + 32, :] = coarse.astype(BF)
+
+    def level_2(h, carry):
+        c = head_lanes(h)
+        k, v = (jnp.concatenate([kv2[t, 0:128, c], kv2[t, 256:384, c]], axis=0) for t in range(2))
+        put(acc2, h * 128, 4.0 * attn(q2[:, c], k, v, half_mask(128, before_on, after_on)))
         return carry
 
-    lax.fori_loop(0, HD, edges, 0)
-    for t in range(2):
-        pooled = dot(fine, kv0[t, 0:128, :]).astype(BF)
-        kv1[t, 64:128, :] = pooled[0:64]
-        kv2[t, 96:128, :] = pooled[64:96]
-        pooled = dot(fine, kv0[t, 640:768, :]).astype(BF)
-        kv1[t, 384:448, :] = pooled[0:64]
-        kv2[t, 256:288, :] = pooled[64:96]
-    for copy in near[2:4]:
-        copy.wait_recv()
+    lax.fori_loop(0, HD, level_2, 0)
+
+    def middle(side, t, n):
+        chunk = n + (2 if side == 0 else 0)
+        coarse = rebuild(rows_of(side, t, 0, chunk, 16), rows_of(side, t, 1, chunk, 16))
+        return rebuild(coarse, rows_of(side, t, 2, n, 32))
+
+    wait_both(near[2])
+    for side in range(2):
+        for t in range(2):
+            for n in range(2):
+                at_row = 384 * side + 64 * n
+                kv1[t, at_row : at_row + 64, :] = middle(side, t, n).astype(BF)
 
     def level_1(h, carry):
-        c = pl.ds(pl.multiple_of(h * E, E), E)
+        c = head_lanes(h)
         for b in range(2):
             mask = half_mask(128, before_on if b == 0 else 1.0, after_on if b == 1 else 1.0)
             k, v = (
@@ -349,32 +361,45 @@
         return carry
 
     lax.fori_loop(0, HD, level_1, 0)
-    for t in range(2):
-        kv2[t, 64:96, :] = dot(coarse, kv1[t, 0:64, :]).astype(BF)
-        kv2[t, 288:320, :] = dot(coarse, kv1[t, 448:512, :]).astype(BF)
-    for copy in near[4:6]:
-        copy.wait_recv()
-
-    def level_2(h, carry):
-        c = pl.ds(pl.multiple_of(h * E, E), E)
-        k, v = (jnp.concatenate([kv2[t, 0:128, c], kv2[t, 256:384, c]], axis=0) for t in range(2))
-        put(acc2, h * 128, 4.0 * attn(q2[:, c], k, v, half_mask(128, before_on, after_on)))
+
+    third.wait_recv()
+    col192 = iota((64, 192), 1)
+    last_on = jnp.where(par == 0, pair_after_on, pair_before_on)
+    mask3 = jnp.where(col192 < 64, pair_before_on, jnp.where(col192 < 128, pair_after_on, last_on))
+
+    def level_3(h, carry):
+        c = head_lanes(h)
+        k, v = (jnp.concatenate([hop2[0, t, :, c], hop2[1, t, :, c], hop3[t, :, c]], axis=0) for t in range(2))
+        put(acc3, h * 64, 8.0 * attn(q3[:, c], k, v, mask3))
         return carry
 
-    lax.fori_loop(0, HD, level_2, 0)
+    lax.fori_loop(0, HD, level_3, 0)
+
+    wait_both(near[3])
+    for side in range(2):
+        for t in range(2):
+            fine = rebuild(middle(side, t, 1 - side), in_near[side, t, 192:256, :].astype(F32))
+            kv0[t, 640 * side : 640 * side + 128, :] = fine.astype(BF)
+
+    def edges(h, carry):
+        c = head_lanes(h)
+        pair = (
+            before_on * attn(qu[0:128, c], kv0[0, 0:128, c], kv0[1, 0:128, c]),
+            after_on * attn(qu[384:512, c], kv0[0, 640:768, c], kv0[1, 640:768, c]),
+        )
+        for n, edge in enumerate(pair):
+            for t in range(2):
+                acc0[t, pl.ds(h * ROWS + 384 * n, 128), :] += edge[:, t * E : (t + 1) * E]
+        return carry
+
+    lax.fori_loop(0, HD, edges, 0)
 
     pltpu.make_async_copy(w_own, w_own, recv.at[7]).wait()
     pltpu.make_async_copy(w_oth, w_oth, recv.at[8]).wait()
-    back3.wait_recv()
 
     def den_of(tile, lo, hi, rows):
         return jnp.broadcast_to(tile[:, lo : lo + 1] + tile[:, hi : hi + 1], (rows, E))
 
-    d3 = w3[:, 2 * E : 3 * E].astype(F32)
-    for i in range(2):
-        here = pl.ds((2 * (1 - par) + i) * 64, 64)
-        acc3[0, here, :] = w3[:, i * E : (i + 1) * E].astype(F32)
-        acc3[1, here, :] = den_of(d3, 64 * i, 64 * i + 32, 64)
     for h in range(HD):
         own, oth = w_own[h].astype(F32), w_oth[h].astype(F32)
         acc4[0, h * 32 : h * 32 + 32, :] = oth[0:32]
@@ -394,7 +419,7 @@
         turned = squares[n * 128 : n * 128 + 128].T
         pw[me, :, n * 128 : n * 128 + 128] = jnp.sum(turned, axis=0, keepdims=True)
     power = []
-    for j in range(1, 8):
+    for j in (4, 3, 5, 2, 6, 1, 7):
         copy = pltpu.make_async_remote_copy(
             src_ref=pw.at[me], dst_ref=pw.at[me], send_sem=pw_send.at[j], recv_sem=pw_recv.at[me],
             device_id=(d, (me + j) % NHEAD), device_id_type=MESH,
@@ -440,32 +465,30 @@
             pltpu.VMEM((2, 512, WIDTH), BF),
             pltpu.VMEM((128, WIDTH), BF),
             pltpu.VMEM((2, 384, WIDTH), BF),
-            pltpu.VMEM((2, 64, 256), BF),
-            pltpu.VMEM((2, 128, 256), BF),
+            pltpu.VMEM((64, WIDTH), BF),
+            pltpu.VMEM((2, 384, WIDTH), BF),
+            pltpu.VMEM((2, 2, 256, WIDTH), BF),
+            pltpu.VMEM((2, 2, 64, WIDTH), BF),
+            pltpu.VMEM((2, 64, WIDTH), BF),
             pltpu.VMEM((4, 160, E), BF),
             pltpu.VMEM((4, 80, E), BF),
             pltpu.VMEM((4, 32, E), BF),
             pltpu.VMEM((4, 64, E), BF),
             pltpu.VMEM((4, 32, E), BF),
             pltpu.VMEM((4, 16, E), BF),
-            pltpu.VMEM((2, 64, 256), BF),
-            pltpu.VMEM((2, 2, 128, 256), BF),
-            pltpu.VMEM((64, 384), BF),
-            pltpu.VMEM((64, 384), BF),
             pltpu.VMEM((4, 32, E), BF),
             pltpu.VMEM((4, 48, E), BF),
             pltpu.VMEM((4, 32, E), BF),
             pltpu.VMEM((4, 48, E), BF),
-            pltpu.VMEM((2, 2, 64, 256), F32),
             pltpu.VMEM((2, HD * 512, E), F32),
             pltpu.VMEM((2, HD * 256, E), F32),
             pltpu.VMEM((2, HD * 128, E), F32),
             pltpu.VMEM((2, HD * 64, E), F32),
             pltpu.VMEM((2, HD * 32, E), F32),
             pltpu.VMEM((NHEAD, 1, ROWS), F32),
-            pltpu.SemaphoreType.DMA((48,)),
+            pltpu.SemaphoreType.DMA((40,)),
             pltpu.SemaphoreType.DMA((10,)),
-            pltpu.SemaphoreType.DMA((6,)),
+            pltpu.SemaphoreType.DMA((11,)),
             pltpu.SemaphoreType.DMA((8,)),
             pltpu.SemaphoreType.DMA((8,)),
             pltpu.SemaphoreType.DMA((5,)),

time: 46.8 us -> 43.8 us (0.936)
  Pallas kernels: 44.8 us -> 41.8 us
    pallas_call x1, Pallas kernels: 44.8 us -> 41.8 us  [on_device(): pl.pallas_call(kernel, out_shape=jax.ShapeDtypeStruct((ROWS, WIDTH), BF),...]
where the time goes in v3:
time: 43.8 us; the launch traced here: 43.7 us
  Pallas kernels  41.8 us (95%)
  local copies, waits for them, and re-layouts  1.87 us (4%)
    pallas_call x1, Pallas kernels, on_device(): pl.pallas_call(kernel, out_shape=jax.ShapeDtypeStruct((ROWS, WIDTH), BF),...  41.8 us
    unnamed x1, local copies, waits for them, and re-layouts  1.87 us

profile of v3, /device:TPU:1, one launch (start us, length us, event | category | flops | bytes accessed | tf_op | source)
XLA Modules:
  0.0 43.7 jit_solution(3170160650764956267)
XLA Ops:
  0.0 41.8 %shard_map.55 = bf16[512,512]{1,0:T(8,128)(2,1)} custom-call(bf16[512,512]{1,0:T(8,128)(2,1)} %q_hbm.1, bf16[512,512]{1,0:T(8,128)(2,1)} %k_hbm.1, bf16[512,512]{1,0:T(8,128)(2,1)} %v_hbm.1, f32[4]{0:T(128)} %scale_hbm.1, f32[1,512]{1,0:T(1,128)} %bitcast.1), custom_call_target="tpu_custom_call" | custom-call | tf_op jit(solution)/shard_map/pallas_call | solution.py:452
  41.8 1.9 %copy.7 = bf16[512,512]{1,0:T(8,128)(2,1)} copy(bf16[512,512]{1,0:T(8,128)(2,1)} %shard_map.55) | data formatting | bytes 1048576

commit v4 on v3

--- a/solution.py
+++ b/solution.py
@@ -136,13 +136,8 @@
     loads[0].wait()
     for c in lanes_of:
         kv0[0, 128:640, c] = unit(k_ref[:, c])
-    loads[2].wait()
-    for c in lanes_of:
-        qu[:, c] = unit(q_ref[:, c])
-    for n in (1, 3, 4):
-        loads[n].wait()
-
-    pools_q = pool_matrix(((128, 1, 0, 1), (64, 2, 0, 1), (32, 3, 0, 1)), 256)
+    loads[1].wait()
+
     pools_kv = jnp.concatenate(
         [pool_matrix(((128, 1, 0, 1), (32, 3, 0, 1)), 256)]
         + [detail_matrix(16, 3, c, 256).astype(BF) for c in range(2)]
@@ -150,6 +145,48 @@
         axis=0,
     )
     finest = detail_matrix(64, 1, 0, 128).astype(BF)
+    for half in range(2):
+        for t in range(2):
+            pooled = dot(pools_kv, kv0[t, half * 256 + 128 : half * 256 + 384, :]).astype(BF)
+            kv1[t, 128 + half * 128 : 256 + half * 128, :] = pooled[0:128]
+            out_near[t, half * 32 : half * 32 + 32, :] = pooled[128:160]
+            out_near[t, 64 + half * 32 : 96 + half * 32, :] = pooled[160:192]
+            out_near[t, 128 + half * 64 : 192 + half * 64, :] = pooled[192:256]
+            edge = 128 + half * 384
+            finest_rows = dot(finest, kv0[t, edge : edge + 128, :]).astype(BF)
+            out_near[t, 256 + half * 64 : 320 + half * 64, :] = finest_rows
+
+    pl.semaphore_wait(bar, 28)
+    started = []
+
+    def start(src, dst, seq, rsem):
+        copy = pltpu.make_async_remote_copy(
+            src_ref=src, dst_ref=dst, send_sem=send.at[len(started)], recv_sem=rsem,
+            device_id=(seq, me), device_id_type=MESH,
+        )
+        copy.start()
+        started.append(copy)
+        return copy
+
+    near = []
+
+    def send_near(n):
+        to_left, to_right = ((0, 0), (64, 64), (128, 192), (256, 320))[n]
+        into = slice(64 * n, 64 * n + 64)
+        near.append((
+            start(out_near.at[:, to_right : to_right + 64], in_near.at[0, :, into], right, near_recv.at[n]),
+            start(out_near.at[:, to_left : to_left + 64], in_near.at[1, :, into], left, near_recv.at[4 + n]),
+        ))
+
+    def wait_both(copies):
+        for copy in copies:
+            copy.wait_recv()
+
+    send_near(0)
+
+    loads[2].wait()
+    for c in lanes_of:
+        qu[:, c] = unit(q_ref[:, c])
     small_q = pool_matrix(((32, 4, 0, 1), (16, 5, 0, 1)), ROWS)
     small_k = pool_matrix(((32, 4, 0, 1), (16, 5, 0, 1), (16, 6, 0, 1)), ROWS)
 
@@ -163,49 +200,6 @@
         small[h, 112:128] = sk[32:48, c].astype(BF)
         small[h, 128:144] = sv[32:48, c].astype(BF)
         small[h, 144:160] = jnp.concatenate([sk[48:56, c], sv[48:56, c]], axis=0).astype(BF)
-    for half in range(2):
-        rows = slice(half * 256, half * 256 + 256)
-        pooled = dot(pools_q, qu[rows, :]).astype(BF)
-        q1[half * 128 : half * 128 + 128, :] = pooled[0:128]
-        q2[half * 64 : half * 64 + 64, :] = pooled[128:192]
-        q3[half * 32 : half * 32 + 32, :] = pooled[192:224]
-        for t in range(2):
-            pooled = dot(pools_kv, kv0[t, half * 256 + 128 : half * 256 + 384, :]).astype(BF)
-            kv1[t, 128 + half * 128 : 256 + half * 128, :] = pooled[0:128]
-            out_near[t, half * 32 : half * 32 + 32, :] = pooled[128:160]
-            out_near[t, 64 + half * 32 : 96 + half * 32, :] = pooled[160:192]
-            out_near[t, 128 + half * 64 : 192 + half * 64, :] = pooled[192:256]
-            edge = 128 + half * 384
-            finest_rows = dot(finest, kv0[t, edge : edge + 128, :]).astype(BF)
-            out_near[t, 256 + half * 64 : 320 + half * 64, :] = finest_rows
-
-    pl.semaphore_wait(bar, 28)
-    started = []
-
-    def start(src, dst, seq, rsem):
-        copy = pltpu.make_async_remote_copy(
-            src_ref=src, dst_ref=dst, send_sem=send.at[len(started)], recv_sem=rsem,
-            device_id=(seq, me), device_id_type=MESH,
-        )
-        copy.start()
-        started.append(copy)
-        return copy
-
-    near = []
-
-    def send_near(n):
-        to_left, to_right = ((0, 0), (64, 64), (128, 192), (256, 320))[n]
-        into = slice(64 * n, 64 * n + 64)
-        near.append((
-            start(out_near.at[:, to_right : to_right + 64], in_near.at[0, :, into], right, near_recv.at[n]),
-            start(out_near.at[:, to_left : to_left + 64], in_near.at[1, :, into], left, near_recv.at[4 + n]),
-        ))
-
-    def wait_both(copies):
-        for copy in copies:
-            copy.wait_recv()
-
-    send_near(0)
     own_copy = pltpu.make_async_copy(small.at[r, 32:112], ra.at[r], recv.at[0])
     own_copy.start()
     for i in range(4):
@@ -217,6 +211,14 @@
         i = (r + j) % 4
         start(small.at[i, 32:112], ra.at[r], at(x, 4 * s + i), recv.at[0])
     send_near(1)
+    pools_q = pool_matrix(((128, 1, 0, 1), (64, 2, 0, 1), (32, 3, 0, 1)), 256)
+    for half in range(2):
+        pooled = dot(pools_q, qu[half * 256 : half * 256 + 256, :]).astype(BF)
+        q1[half * 128 : half * 128 + 128, :] = pooled[0:128]
+        q2[half * 64 : half * 64 + 64, :] = pooled[128:192]
+        q3[half * 32 : half * 32 + 32, :] = pooled[192:224]
+    for n in (3, 4):
+        loads[n].wait()
 
     def own_level(h, carry):
         c = pl.ds(pl.multiple_of(h * E, E), E)
@@ -375,6 +377,59 @@
 
     lax.fori_loop(0, HD, level_3, 0)
 
+    pltpu.make_async_copy(w_own, w_own, recv.at[7]).wait()
+    pltpu.make_async_copy(w_oth, w_oth, recv.at[8]).wait()
+
+    def den_of(tile, lo, hi, rows):
+        return jnp.broadcast_to(tile[:, lo : lo + 1] + tile[:, hi : hi + 1], (rows, E))
+
+    for h in range(HD):
+        own, oth = w_own[h].astype(F32), w_oth[h].astype(F32)
+        acc4[0, h * 32 : h * 32 + 32, :] = oth[0:32]
+        acc4[1, h * 32 : h * 32 + 16, :] = den_of(oth[32:48], 0, 16, 16)
+        acc4[1, h * 32 + 16 : h * 32 + 32, :] = den_of(oth[32:48], 32, 48, 16)
+        spread(acc4, (own[0:16], den_of(own[16:32], 0, 16, 16)), h, 16)
+        for acc, finer, n in ((acc4, acc3, 32), (acc3, acc2, 64), (acc2, acc1, 128), (acc1, acc0, 256)):
+            spread(finer, tuple(acc[t, h * n : h * n + n, :] for t in range(2)), h, n)
+
+    power = []
+
+    def share_power(part, starts):
+        for n, first in enumerate(starts):
+            squares = jnp.zeros((128, E), F32)
+            for h in range(HD):
+                rows = slice(h * ROWS + first, h * ROWS + first + 128)
+                scaled = acc0[0, rows, :] / acc0[1, rows, :] * scale_ref[h]
+                acc0[0, rows, :] = scaled
+                squares = squares + scaled * scaled
+            pw[part, me, :, n * 128 : n * 128 + 128] = jnp.sum(squares.T, axis=0, keepdims=True)
+        for j in (4, 3, 5, 2, 6, 1, 7):
+            copy = pltpu.make_async_remote_copy(
+                src_ref=pw.at[part, me], dst_ref=pw.at[part, me],
+                send_sem=pw_send.at[part, j], recv_sem=pw_recv.at[part, me],
+                device_id=(d, (me + j) % NHEAD), device_id_type=MESH,
+            )
+            copy.start()
+            power.append(copy)
+
+    def write_out(part, starts):
+        for j in range(1, 8):
+            peer = (me + j) % NHEAD
+            pltpu.make_async_remote_copy(
+                src_ref=pw.at[part, peer], dst_ref=pw.at[part, peer],
+                send_sem=pw_send.at[part, j], recv_sem=pw_recv.at[part, peer],
+                device_id=(d, peer), device_id_type=MESH,
+            ).wait_recv()
+        total = jnp.sum(pw[part], axis=0)
+        factor = lax.rsqrt(total / (NHEAD * WIDTH) + EPSILON)
+        for n, first in enumerate(starts):
+            column = jnp.broadcast_to(factor[:, n * 128 : n * 128 + 128], (128, 128)).T
+            for h, c in enumerate(lanes_of):
+                scaled = acc0[0, h * ROWS + first : h * ROWS + first + 128, :]
+                o_ref[first : first + 128, c] = (scaled * column * gain_ref[:, c]).astype(BF)
+
+    share_power(0, (128, 256))
+
     wait_both(near[3])
     for side in range(2):
         for t in range(2):
@@ -393,53 +448,9 @@
         return carry
 
     lax.fori_loop(0, HD, edges, 0)
-
-    pltpu.make_async_copy(w_own, w_own, recv.at[7]).wait()
-    pltpu.make_async_copy(w_oth, w_oth, recv.at[8]).wait()
-
-    def den_of(tile, lo, hi, rows):
-        return jnp.broadcast_to(tile[:, lo : lo + 1] + tile[:, hi : hi + 1], (rows, E))
-
-    for h in range(HD):
-        own, oth = w_own[h].astype(F32), w_oth[h].astype(F32)
-        acc4[0, h * 32 : h * 32 + 32, :] = oth[0:32]
-        acc4[1, h * 32 : h * 32 + 16, :] = den_of(oth[32:48], 0, 16, 16)
-        acc4[1, h * 32 + 16 : h * 32 + 32, :] = den_of(oth[32:48], 32, 48, 16)
-        spread(acc4, (own[0:16], den_of(own[16:32], 0, 16, 16)), h, 16)
-        for acc, finer, n in ((acc4, acc3, 32), (acc3, acc2, 64), (acc2, acc1, 128), (acc1, acc0, 256)):
-            spread(finer, tuple(acc[t, h * n : h * n + n, :] for t in range(2)), h, n)
-
-    squares = jnp.zeros((ROWS, E), F32)
-    for h in range(HD):
-        rows = slice(h * ROWS, (h + 1) * ROWS)
-        scaled = acc0[0, rows, :] / acc0[1, rows, :] * scale_ref[h]
-        acc0[0, rows, :] = scaled
-        squares = squares + scaled * scaled
-    for n in range(4):
-        turned = squares[n * 128 : n * 128 + 128].T
-        pw[me, :, n * 128 : n * 128 + 128] = jnp.sum(turned, axis=0, keepdims=True)
-    power = []
-    for j in (4, 3, 5, 2, 6, 1, 7):
-        copy = pltpu.make_async_remote_copy(
-            src_ref=pw.at[me], dst_ref=pw.at[me], send_sem=pw_send.at[j], recv_sem=pw_recv.at[me],
-            device_id=(d, (me + j) % NHEAD), device_id_type=MESH,
-        )
-        copy.start()
-        power.append(copy)
-    for j in range(1, 8):
-        peer = (me + j) % NHEAD
-        pltpu.make_async_remote_copy(
-            src_ref=pw.at[peer], dst_ref=pw.at[peer], send_sem=pw_send.at[j], recv_sem=pw_recv.at[peer],
-            device_id=(d, peer), device_id_type=MESH,
-        ).wait_recv()
-    total = jnp.sum(pw[...], axis=0)
-    factor = lax.rsqrt(total / (NHEAD * WIDTH) + EPSILON)
-    for n in range(4):
-        column = jnp.broadcast_to(factor[:, n * 128 : n * 128 + 128], (128, 128)).T
-        for h in range(HD):
-            c = slice(h * E, (h + 1) * E)
-            scaled = acc0[0, h * ROWS + n * 128 : h * ROWS + n * 128 + 128, :]
-            o_ref[n * 128 : n * 128 + 128, c] = (scaled * column * gain_ref[:, c]).astype(BF)
+    share_power(1, (0, 384))
+    write_out(0, (128, 256))
+    write_out(1, (0, 384))
     for copy in started:
         copy.wait_send()
     for copy in power:
@@ -485,16 +496,16 @@
             pltpu.VMEM((2, HD * 128, E), F32),
             pltpu.VMEM((2, HD * 64, E), F32),
             pltpu.VMEM((2, HD * 32, E), F32),
-            pltpu.VMEM((NHEAD, 1, ROWS), F32),
+            pltpu.VMEM((2, NHEAD, 1, ROWS // 2), F32),
             pltpu.SemaphoreType.DMA((40,)),
             pltpu.SemaphoreType.DMA((10,)),
             pltpu.SemaphoreType.DMA((11,)),
-            pltpu.SemaphoreType.DMA((8,)),
-            pltpu.SemaphoreType.DMA((8,)),
+            pltpu.SemaphoreType.DMA((2, 8)),
+            pltpu.SemaphoreType.DMA((2, 8)),
             pltpu.SemaphoreType.DMA((5,)),
         ],
         compiler_params=pltpu.CompilerParams(
-            collective_id=0, has_side_effects=True, vmem_limit_bytes=60 * 2**20
+            collective_id=0, has_side_effects=True, vmem_limit_bytes=int(53.25 * 2**20)
         ),
     )(queries, key_inputs, value_inputs, head_scale, out_gain.reshape(1, WIDTH))
 

time: 43.8 us -> 43.1 us (0.984)
  Pallas kernels: 41.8 us -> 40.8 us
    pallas_call x1, Pallas kernels: 41.8 us -> 40.8 us  [on_device(): pl.pallas_call(kernel, out_shape=jax.ShapeDtypeStruct((ROWS, WIDTH), BF),...]
    unnamed x1 -> x5, local copies, waits for them, and re-layouts: 1.87 us -> 2.13 us
where the time goes in v4:
time: 43.1 us; the launch traced here: 42.9 us
  Pallas kernels  40.8 us (95%)
  local copies, waits for them, and re-layouts  2.13 us (5%)
    pallas_call x1, Pallas kernels, on_device(): pl.pallas_call(kernel, out_shape=jax.ShapeDtypeStruct((ROWS, WIDTH), BF),...  40.8 us
    unnamed x5, local copies, waits for them, and re-layouts  2.13 us

profile of v4, /device:TPU:1, one launch (start us, length us, event | category | flops | bytes accessed | tf_op | source)
XLA Modules:
  0.0 42.9 jit_solution(17217199119526864309)
XLA Ops:
  0.0 0.0 copy-start.1
  0.0 0.7 %copy-done.1 = f32[4]{0:T(128)S(1)} copy-done((f32[4]{0:T(128)S(1)}, f32[4]{0:T(128)}, u32[]{:S(2)}) %copy-start.1) | copy-done | bytes 40
  0.7 0.0 copy-start
  0.7 0.7 %copy-done = f32[512]{0:T(512)S(1)} copy-done((f32[512]{0:T(512)S(1)}, f32[512]{0:T(512)}, u32[]{:S(2)}) %copy-start) | copy-done | bytes 2072
  1.3 40.8 %shard_map.55 = bf16[512,512]{1,0:T(8,128)(2,1)S(1)} custom-call(bf16[512,512]{1,0:T(8,128)(2,1)} %q_hbm.1, bf16[512,512]{1,0:T(8,128)(2,1)} %k_hbm.1, bf16[512,512]{1,0:T(8,128)(2,1)} %v_hbm.1, f32[4]{0:T(128)S(1)} %copy-done.1, f32[1,512]{1,0:T(1,128)S(1)} %bitcast.1), custom_call_target="tpu_custom_call" | custom-call | tf_op jit(solution)/shard_map/pallas_call | solution.py:463
  42.1 0.8 %copy.7 = bf16[512,512]{1,0:T(8,128)(2,1)} copy(bf16[512,512]{1,0:T(8,128)(2,1)S(1)} %shard_map.55) | data formatting | bytes 1048576
Async XLA Ops:
  0.0 0.7 %copy-start.1 = (f32[4]{0:T(128)S(1)}, f32[4]{0:T(128)}, u32[]{:S(2)}) copy-start(f32[4]{0:T(128)} %scale_hbm.1) | copy-start | bytes 52
  0.7 0.7 %copy-start = (f32[512]{0:T(512)S(1)}, f32[512]{0:T(512)}, u32[]{:S(2)}) copy-start(f32[512]{0:T(512)} %param.9) | copy-start | bytes 6148

commit v5 on v4

--- a/solution.py
+++ b/solution.py
@@ -1,3 +1,5 @@
+import math
+
 import jax
 import jax.numpy as jnp
 from jax import lax
@@ -13,7 +15,7 @@
 ROWS = 512
 HD = 4
 WIDTH = HD * E
-SCALE = E ** (-0.5)
+SCALE = E ** (-0.5) * math.log2(math.e)
 NX, NZ, NSEQ, NHEAD = 4, 8, 32, 8
 
 
@@ -48,13 +50,17 @@
     return jnp.dot(a, b, preferred_element_type=F32)
 
 
+def attn_all(jobs):
+    logits = [
+        lax.dot_general(q, k, (((1,), (1,)), ((), ())), preferred_element_type=F32) for q, k, v, mask in jobs
+    ]
+    weights = [jnp.exp2(x * SCALE) for x in logits]
+    weights = [(p if job[3] is None else p * job[3]).astype(BF) for p, job in zip(weights, jobs)]
+    return [dot(p, jnp.concatenate([job[2], jnp.ones(job[2].shape, BF)], axis=1)) for p, job in zip(weights, jobs)]
+
+
 def attn(q, k, v, mask=None):
-    logits = lax.dot_general(q, k, (((1,), (1,)), ((), ())), preferred_element_type=F32)
-    p = jnp.exp(logits * SCALE)
-    if mask is not None:
-        p = p * mask
-    va = jnp.concatenate([v, jnp.ones(v.shape, BF)], axis=1)
-    return dot(p.astype(BF), va)
+    return attn_all([(q, k, v, mask)])[0]
 
 
 def half_mask(rows, before_on, after_on):
@@ -108,15 +114,6 @@
     def at(row, col):
         return row * NZ + col
 
-    loads = [
-        pltpu.make_async_copy(src, dst, load.at[n])
-        for n, (src, dst) in enumerate((
-            (k_hbm, k_ref), (v_hbm, kv0.at[1, 128:640]), (q_hbm, q_ref), (scale_hbm, scale_ref), (gain_hbm, gain_ref)
-        ))
-    ]
-    for copy in loads:
-        copy.start()
-
     bar = pltpu.get_barrier_semaphore()
 
     def signal(seq, head):
@@ -131,6 +128,15 @@
         signal(at(x_far, 4 * s + i), me)
     signal(left, me)
     signal(right, me)
+
+    loads = [
+        pltpu.make_async_copy(src, dst, load.at[n])
+        for n, (src, dst) in enumerate((
+            (k_hbm, k_ref), (v_hbm, kv0.at[1, 128:640]), (q_hbm, q_ref), (scale_hbm, scale_ref), (gain_hbm, gain_ref)
+        ))
+    ]
+    for copy in loads:
+        copy.start()
 
     lanes_of = [slice(h * E, (h + 1) * E) for h in range(HD)]
     loads[0].wait()
@@ -220,22 +226,27 @@
     for n in (3, 4):
         loads[n].wait()
 
-    def own_level(h, carry):
-        c = pl.ds(pl.multiple_of(h * E, E), E)
-        for b in range(4):
-            lo, hi = max(b - 1, 0), min(b + 2, 4)
-            keys = slice(128 + lo * 128, 128 + hi * 128)
-            put(acc0, h * ROWS + b * 128, attn(qu[b * 128 : b * 128 + 128, c], kv0[0, keys, c], kv0[1, keys, c]))
-        return carry
-
-    lax.fori_loop(0, 2, own_level, 0)
+    def own_level(heads):
+        jobs, places = [], []
+        for h in heads:
+            c = lanes_of[h]
+            for b in range(4):
+                keys = slice(128 + max(b - 1, 0) * 128, 128 + min(b + 2, 4) * 128)
+                jobs.append((qu[b * 128 : b * 128 + 128, c], kv0[0, keys, c], kv0[1, keys, c], None))
+                places.append(h * ROWS + b * 128)
+        for place, out in zip(places, attn_all(jobs)):
+            put(acc0, place, out)
+
+    own_level((0,))
+    own_level((1,))
     wait_both(near[0])
     second = (
         start(in_near.at[0, :, 0:64], hop2.at[0], right, near_recv.at[8]),
         start(in_near.at[1, :, 0:64], hop2.at[1], left, near_recv.at[9]),
     )
     send_near(2)
-    lax.fori_loop(2, HD, own_level, 0)
+    own_level((2,))
+    own_level((3,))
 
     for n, ref in enumerate((ra, rb, rc, rd, re)):
         pltpu.make_async_copy(ref, ref, recv.at[n]).wait()
@@ -261,7 +272,7 @@
     sign = 2 * s - 1
     lead = (kh - qh) * sign
     mask4 = jnp.where(
-        col < 128, jnp.where(lead >= 0, 1.0, 0.0), jnp.where(lead <= 0, 1.0 - wrap, 0.0)
+        col < 128, jnp.where(lead >= 0, 16.0, 0.0), jnp.where(lead <= 0, 16.0 - 16.0 * wrap, 0.0)
     )
     k5 = jnp.concatenate([pooled_c[0:64, 0:E], kv_d[:, 0:E]], axis=0)
     v5 = jnp.concatenate([pooled_c[0:64, E:], kv_d[:, E:]], axis=0)
@@ -273,14 +284,17 @@
         [jnp.concatenate([far[i, 8:16] for i in range(4)], axis=0).astype(BF), pooled_c[64:96, E:], pooled_d[:, E:]], axis=0
     )
     col6 = iota((128, 96), 1)
-    mask6 = jnp.where(col6 < 32, 1.0, jnp.where(col6 < 64, wrap, wrap_d))
-    mask5 = jnp.where(iota((64, 128), 1) < 64, 1.0 - wrap, 1.0 - wrap_d)
-    out_own = 32.0 * attn(q5, k5, v5, mask5) + 64.0 * attn(q6, k6, v6, mask6[0:64])
-    out_oth = (
-        16.0 * attn(q4, k4, v4, mask4)
-        + 32.0 * (1.0 - wrap_d) * attn(q_oth[0:128], kv_d[:, 0:E], kv_d[:, E:])
-        + 64.0 * attn(q_oth[128:256], k6, v6, mask6)
-    )
+    mask6 = 64.0 * jnp.where(col6 < 32, 1.0, jnp.where(col6 < 64, wrap, wrap_d))
+    mask5 = 32.0 * jnp.where(iota((64, 128), 1) < 64, 1.0 - wrap, 1.0 - wrap_d)
+    outs = attn_all([
+        (q4, k4, v4, mask4),
+        (q5, k5, v5, mask5),
+        (q6, k6, v6, mask6[0:64]),
+        (q_oth[0:128], kv_d[:, 0:E], kv_d[:, E:], None),
+        (q_oth[128:256], k6, v6, mask6),
+    ])
+    out_own = outs[1] + outs[2]
+    out_oth = outs[0] + 32.0 * (1.0 - wrap_d) * outs[3] + outs[4]
 
     lane = iota((16, E), 1)
 
@@ -315,9 +329,6 @@
     third = start(hop2.at[par], hop3, 2 * g + 1 - par, near_recv.at[10])
     send_near(3)
 
-    def head_lanes(h):
-        return pl.ds(pl.multiple_of(h * E, E), E)
-
     def rows_of(side, t, n, chunk, rows):
         return in_near[side, t, 64 * n + rows * chunk : 64 * n + rows * chunk + rows, :].astype(F32)
 
@@ -329,13 +340,15 @@
                 at_row = 256 * side + 32 * chunk
                 kv2[t, at_row : at_row + 32, :] = coarse.astype(BF)
 
-    def level_2(h, carry):
-        c = head_lanes(h)
-        k, v = (jnp.concatenate([kv2[t, 0:128, c], kv2[t, 256:384, c]], axis=0) for t in range(2))
-        put(acc2, h * 128, 4.0 * attn(q2[:, c], k, v, half_mask(128, before_on, after_on)))
-        return carry
-
-    lax.fori_loop(0, HD, level_2, 0)
+    def pair_rows(kv, t, first, second, c):
+        return jnp.concatenate([kv[t, first : first + 128, c], kv[t, second : second + 128, c]], axis=0)
+
+    mask2 = 4.0 * half_mask(128, before_on, after_on)
+    outs = attn_all([
+        (q2[:, c], pair_rows(kv2, 0, 0, 256, c), pair_rows(kv2, 1, 0, 256, c), mask2) for c in lanes_of
+    ])
+    for h, out in enumerate(outs):
+        put(acc2, h * 128, out)
 
     def middle(side, t, n):
         chunk = n + (2 if side == 0 else 0)
@@ -349,33 +362,28 @@
                 at_row = 384 * side + 64 * n
                 kv1[t, at_row : at_row + 64, :] = middle(side, t, n).astype(BF)
 
-    def level_1(h, carry):
-        c = head_lanes(h)
-        for b in range(2):
-            mask = half_mask(128, before_on if b == 0 else 1.0, after_on if b == 1 else 1.0)
-            k, v = (
-                jnp.concatenate(
-                    [kv1[t, b * 128 : b * 128 + 128, c], kv1[t, 256 + b * 128 : 384 + b * 128, c]], axis=0
-                )
-                for t in range(2)
-            )
-            put(acc1, h * 256 + b * 128, 2.0 * attn(q1[b * 128 : b * 128 + 128, c], k, v, mask))
-        return carry
-
-    lax.fori_loop(0, HD, level_1, 0)
+    masks1 = (2.0 * half_mask(128, before_on, 1.0), 2.0 * half_mask(128, 1.0, after_on))
+    for b, mask1 in enumerate(masks1):
+        lo, hi = b * 128, 256 + b * 128
+        outs = attn_all([
+            (q1[lo : lo + 128, c], pair_rows(kv1, 0, lo, hi, c), pair_rows(kv1, 1, lo, hi, c), mask1) for c in lanes_of
+        ])
+        for h, out in enumerate(outs):
+            put(acc1, h * 256 + b * 128, out)
 
     third.wait_recv()
     col192 = iota((64, 192), 1)
     last_on = jnp.where(par == 0, pair_after_on, pair_before_on)
-    mask3 = jnp.where(col192 < 64, pair_before_on, jnp.where(col192 < 128, pair_after_on, last_on))
-
-    def level_3(h, carry):
-        c = head_lanes(h)
-        k, v = (jnp.concatenate([hop2[0, t, :, c], hop2[1, t, :, c], hop3[t, :, c]], axis=0) for t in range(2))
-        put(acc3, h * 64, 8.0 * attn(q3[:, c], k, v, mask3))
-        return carry
-
-    lax.fori_loop(0, HD, level_3, 0)
+    mask3 = 8.0 * jnp.where(col192 < 64, pair_before_on, jnp.where(col192 < 128, pair_after_on, last_on))
+
+    outs = attn_all([
+        (q3[:, c],)
+        + tuple(jnp.concatenate([hop2[0, n, :, c], hop2[1, n, :, c], hop3[n, :, c]], axis=0) for n in range(2))
+        + (mask3,)
+        for c in lanes_of
+    ])
+    for h, out in enumerate(outs):
+        put(acc3, h * 64, out)
 
     pltpu.make_async_copy(w_own, w_own, recv.at[7]).wait()
     pltpu.make_async_copy(w_oth, w_oth, recv.at[8]).wait()
@@ -436,18 +444,16 @@
             fine = rebuild(middle(side, t, 1 - side), in_near[side, t, 192:256, :].astype(F32))
             kv0[t, 640 * side : 640 * side + 128, :] = fine.astype(BF)
 
-    def edges(h, carry):
-        c = head_lanes(h)
-        pair = (
-            before_on * attn(qu[0:128, c], kv0[0, 0:128, c], kv0[1, 0:128, c]),
-            after_on * attn(qu[384:512, c], kv0[0, 640:768, c], kv0[1, 640:768, c]),
-        )
-        for n, edge in enumerate(pair):
-            for t in range(2):
-                acc0[t, pl.ds(h * ROWS + 384 * n, 128), :] += edge[:, t * E : (t + 1) * E]
-        return carry
-
-    lax.fori_loop(0, HD, edges, 0)
+    ends = ((0, 0, before_on), (384, 640, after_on))
+    outs = attn_all([
+        (qu[first : first + 128, c], kv0[0, key : key + 128, c], kv0[1, key : key + 128, c], None)
+        for c in lanes_of
+        for first, key, on in ends
+    ])
+    for n, out in enumerate(outs):
+        first, key, on = ends[n % 2]
+        for t in range(2):
+            acc0[t, pl.ds(n // 2 * ROWS + first, 128), :] += on * out[:, t * E : (t + 1) * E]
     share_power(1, (0, 384))
     write_out(0, (128, 256))
     write_out(1, (0, 384))

time: 43.1 us -> 41.2 us (0.956)
  Pallas kernels: 40.8 us -> 38.9 us
    pallas_call x1, Pallas kernels: 40.8 us -> 38.9 us  [on_device(): pl.pallas_call(kernel, out_shape=jax.ShapeDtypeStruct((ROWS, WIDTH), BF),...]
where the time goes in v5:
time: 41.2 us; the launch traced here: 41.1 us
  Pallas kernels  38.9 us (94%)
  local copies, waits for them, and re-layouts  2.13 us (5%)
    pallas_call x1, Pallas kernels, on_device(): pl.pallas_call(kernel, out_shape=jax.ShapeDtypeStruct((ROWS, WIDTH), BF),...  38.9 us
    unnamed x5, local copies, waits for them, and re-layouts  2.13 us

profile of v5, /device:TPU:1, one launch (start us, length us, event | category | flops | bytes accessed | tf_op | source)
XLA Modules:
  0.0 41.1 jit_solution(4426678588103892027)
XLA Ops:
  0.0 0.0 copy-start.1
  0.0 0.7 %copy-done.1 = f32[4]{0:T(128)S(1)} copy-done((f32[4]{0:T(128)S(1)}, f32[4]{0:T(128)}, u32[]{:S(2)}) %copy-start.1) | copy-done | bytes 40
  0.7 0.0 copy-start
  0.7 0.7 %copy-done = f32[512]{0:T(512)S(1)} copy-done((f32[512]{0:T(512)S(1)}, f32[512]{0:T(512)}, u32[]{:S(2)}) %copy-start) | copy-done | bytes 2072
  1.3 38.9 %shard_map.55 = bf16[512,512]{1,0:T(8,128)(2,1)S(1)} custom-call(bf16[512,512]{1,0:T(8,128)(2,1)} %q_hbm.1, bf16[512,512]{1,0:T(8,128)(2,1)} %k_hbm.1, bf16[512,512]{1,0:T(8,128)(2,1)} %v_hbm.1, f32[4]{0:T(128)S(1)} %copy-done.1, f32[1,512]{1,0:T(1,128)S(1)} %bitcast.1), custom_call_target="tpu_custom_call" | custom-call | tf_op jit(solution)/shard_map/pallas_call | solution.py:469
  40.3 0.8 %copy.7 = bf16[512,512]{1,0:T(8,128)(2,1)} copy(bf16[512,512]{1,0:T(8,128)(2,1)S(1)} %shard_map.55) | data formatting | bytes 1048576
Async XLA Ops:
  0.0 0.7 %copy-start.1 = (f32[4]{0:T(128)S(1)}, f32[4]{0:T(128)}, u32[]{:S(2)}) copy-start(f32[4]{0:T(128)} %scale_hbm.1) | copy-start | bytes 52
  0.7 0.7 %copy-start = (f32[512]{0:T(512)S(1)}, f32[512]{0:T(512)}, u32[]{:S(2)}) copy-start(f32[512]{0:T(512)} %param.9) | copy-start | bytes 6148

commit v6 on v5

--- a/solution.py
+++ b/solution.py
@@ -96,8 +96,8 @@
 
 
 def kernel(
-    q_hbm, k_hbm, v_hbm, scale_hbm, gain_hbm, o_ref,
-    q_ref, k_ref, scale_ref, gain_ref, qu, kv0, q1, kv1, q2, kv2, q3, out_near, in_near, hop2, hop3, small, ra, rb, rc, rd, re,
+    q_hbm, k_hbm, v_hbm, scale_hbm, o_ref,
+    q_ref, k_ref, scale_ref, qu, kv0, q1, kv1, q2, kv2, q3, out_near, in_near, hop2, hop3, small, ra, rb, rc, rd, re,
     u_own, u_oth, w_own, w_oth,
     acc0, acc1, acc2, acc3, acc4, pw, send, recv, near_recv, pw_send, pw_recv, load,
 ):
@@ -132,7 +132,7 @@
     loads = [
         pltpu.make_async_copy(src, dst, load.at[n])
         for n, (src, dst) in enumerate((
-            (k_hbm, k_ref), (v_hbm, kv0.at[1, 128:640]), (q_hbm, q_ref), (scale_hbm, scale_ref), (gain_hbm, gain_ref)
+            (k_hbm, k_ref), (v_hbm, kv0.at[1, 128:640]), (q_hbm, q_ref), (scale_hbm, scale_ref)
         ))
     ]
     for copy in loads:
@@ -223,8 +223,7 @@
         q1[half * 128 : half * 128 + 128, :] = pooled[0:128]
         q2[half * 64 : half * 64 + 64, :] = pooled[128:192]
         q3[half * 32 : half * 32 + 32, :] = pooled[192:224]
-    for n in (3, 4):
-        loads[n].wait()
+    loads[3].wait()
 
     def own_level(heads):
         jobs, places = [], []
@@ -434,7 +433,7 @@
             column = jnp.broadcast_to(factor[:, n * 128 : n * 128 + 128], (128, 128)).T
             for h, c in enumerate(lanes_of):
                 scaled = acc0[0, h * ROWS + first : h * ROWS + first + 128, :]
-                o_ref[first : first + 128, c] = (scaled * column * gain_ref[:, c]).astype(BF)
+                o_ref[first : first + 128, c] = (scaled * column).astype(BF)
 
     share_power(0, (128, 256))
 
@@ -466,16 +465,15 @@
 def on_device(queries, key_inputs, value_inputs, head_scale, out_gain):
     vmem = pl.BlockSpec(memory_space=pltpu.VMEM)
     hbm = pl.BlockSpec(memory_space=pltpu.HBM)
-    return pl.pallas_call(
+    normed = pl.pallas_call(
         kernel,
         out_shape=jax.ShapeDtypeStruct((ROWS, WIDTH), BF),
-        in_specs=[hbm] * 5,
+        in_specs=[hbm] * 4,
         out_specs=vmem,
         scratch_shapes=[
             pltpu.VMEM((512, WIDTH), BF),
             pltpu.VMEM((512, WIDTH), BF),
             pltpu.SMEM((HD,), F32),
-            pltpu.VMEM((1, WIDTH), F32),
             pltpu.VMEM((512, WIDTH), BF),
             pltpu.VMEM((2, 768, WIDTH), BF),
             pltpu.VMEM((256, WIDTH), BF),
@@ -513,7 +511,8 @@
         compiler_params=pltpu.CompilerParams(
             collective_id=0, has_side_effects=True, vmem_limit_bytes=int(53.25 * 2**20)
         ),
-    )(queries, key_inputs, value_inputs, head_scale, out_gain.reshape(1, WIDTH))
+    )(queries, key_inputs, value_inputs, head_scale)
+    return (normed.astype(F32) * out_gain[None, :]).astype(BF)
 
 
 def solution(mesh):

time: 41.2 us -> 40.6 us (0.985)
  local copies, waits for them, and re-layouts: 2.13 us -> 0.66 us
  other arithmetic: 0 us -> 0.89 us
    unnamed x5 -> x4, local copies, waits for them, and re-layouts: 2.13 us -> 0.66 us
    convert_element_type x0 -> x1, other arithmetic: none -> 0.89 us  [on_device(): return (normed.astype(F32) * out_gain[None, :]).astype(BF)]
where the time goes in v6:
time: 40.6 us; the launch traced here: 40.5 us
  Pallas kernels  38.9 us (96%)
  other arithmetic  0.89 us (2%)
  local copies, waits for them, and re-layouts  0.66 us (2%)
    pallas_call x1, Pallas kernels, on_device(): pl.pallas_call(kernel, out_shape=jax.ShapeDtypeStruct((ROWS, WIDTH), BF),...  38.9 us
    convert_element_type x1, other arithmetic, on_device(): return (normed.astype(F32) * out_gain[None, :]).astype(BF)  0.89 us

profile of v6, /device:TPU:1, one launch (start us, length us, event | category | flops | bytes accessed | tf_op | source)
XLA Modules:
  0.0 40.5 jit_solution(11237009118897612409)
XLA Ops:
  0.0 0.0 copy-start
  0.0 0.7 %copy-done = f32[4]{0:T(128)S(1)} copy-done((f32[4]{0:T(128)S(1)}, f32[4]{0:T(128)}, u32[]{:S(2)}) %copy-start) | copy-done | bytes 40
  0.7 0.0 copy-start.1
  0.7 38.9 %shard_map.55 = bf16[512,512]{1,0:T(8,128)(2,1)S(1)} custom-call(bf16[512,512]{1,0:T(8,128)(2,1)} %q_hbm.1, bf16[512,512]{1,0:T(8,128)(2,1)} %k_hbm.1, bf16[512,512]{1,0:T(8,128)(2,1)} %v_hbm.1, f32[4]{0:T(128)S(1)} %copy-done), custom_call_target="tpu_custom_call" | custom-call | tf_op jit(solution)/shard_map/pallas_call | solution.py:468
  39.6 0.0 copy-done.1
  39.6 0.9 %multiply_convert_fusion = bf16[512,512]{1,0:T(8,128)(2,1)} fusion(bf16[512,512]{1,0:T(8,128)(2,1)S(1)} %shard_map.55, f32[512]{0:T(512)S(1)} %copy-done.1), kind=kLoop, calls=%fused_computation | loop fusion | flops 786432 | bytes 1050624 | tf_op jit(solution)/shard_map/convert_element_type | solution.py:515
Async XLA Ops:
  0.0 0.7 %copy-start = (f32[4]{0:T(128)S(1)}, f32[4]{0:T(128)}, u32[]{:S(2)}) copy-start(f32[4]{0:T(128)} %scale_hbm.1) | copy-start | bytes 52
  0.7 38.9 %copy-start.1 = (f32[512]{0:T(512)S(1)}, f32[512]{0:T(512)}, u32[]{:S(2)}) copy-start(f32[512]{0:T(512)} %param.9) | copy-start | bytes 6148

commit v7 on v6

--- a/solution.py
+++ b/solution.py
@@ -216,7 +216,6 @@
     for j in range(1, 4):
         i = (r + j) % 4
         start(small.at[i, 32:112], ra.at[r], at(x, 4 * s + i), recv.at[0])
-    send_near(1)
     pools_q = pool_matrix(((128, 1, 0, 1), (64, 2, 0, 1), (32, 3, 0, 1)), 256)
     for half in range(2):
         pooled = dot(pools_q, qu[half * 256 : half * 256 + 256, :]).astype(BF)
@@ -243,6 +242,7 @@
         start(in_near.at[0, :, 0:64], hop2.at[0], right, near_recv.at[8]),
         start(in_near.at[1, :, 0:64], hop2.at[1], left, near_recv.at[9]),
     )
+    send_near(1)
     send_near(2)
     own_level((2,))
     own_level((3,))
@@ -312,13 +312,13 @@
         other = out_oth[i * 32 : i * 32 + 32]
         u_oth[i, 0:32] = other[:, 0:E].astype(BF)
         u_oth[i, 32:48] = den_tile([other[0:16, E:], other[16:32, E:]])
+    for i in range(4):
+        start(u_oth.at[i], w_oth.at[r], at(x, 4 * (1 - s) + i), recv.at[8])
     own_return = pltpu.make_async_copy(u_own.at[r], w_own.at[r], recv.at[7])
     own_return.start()
     for j in range(1, 4):
         i = (r + j) % 4
         start(u_own.at[i], w_own.at[r], at(x, 4 * s + i), recv.at[7])
-    for i in range(4):
-        start(u_oth.at[i], w_oth.at[r], at(x, 4 * (1 - s) + i), recv.at[8])
 
     before_on = jnp.where(d >= 1, 1.0, 0.0)
     after_on = jnp.where(d <= NSEQ - 2, 1.0, 0.0)
@@ -435,8 +435,6 @@
                 scaled = acc0[0, h * ROWS + first : h * ROWS + first + 128, :]
                 o_ref[first : first + 128, c] = (scaled * column).astype(BF)
 
-    share_power(0, (128, 256))
-
     wait_both(near[3])
     for side in range(2):
         for t in range(2):
@@ -453,9 +451,8 @@
         first, key, on = ends[n % 2]
         for t in range(2):
             acc0[t, pl.ds(n // 2 * ROWS + first, 128), :] += on * out[:, t * E : (t + 1) * E]
-    share_power(1, (0, 384))
-    write_out(0, (128, 256))
-    write_out(1, (0, 384))
+    share_power(0, (0, 128, 256, 384))
+    write_out(0, (0, 128, 256, 384))
     for copy in started:
         copy.wait_send()
     for copy in power:
@@ -500,12 +497,12 @@
             pltpu.VMEM((2, HD * 128, E), F32),
             pltpu.VMEM((2, HD * 64, E), F32),
             pltpu.VMEM((2, HD * 32, E), F32),
-            pltpu.VMEM((2, NHEAD, 1, ROWS // 2), F32),
+            pltpu.VMEM((1, NHEAD, 1, ROWS), F32),
             pltpu.SemaphoreType.DMA((40,)),
             pltpu.SemaphoreType.DMA((10,)),
             pltpu.SemaphoreType.DMA((11,)),
-            pltpu.SemaphoreType.DMA((2, 8)),
-            pltpu.SemaphoreType.DMA((2, 8)),
+            pltpu.SemaphoreType.DMA((1, 8)),
+            pltpu.SemaphoreType.DMA((1, 8)),
             pltpu.SemaphoreType.DMA((5,)),
         ],
         compiler_params=pltpu.CompilerParams(

time: 40.6 us -> 40.5 us (level)
  no operation moved by 1% of the time
where the time goes in v7:
time: 40.5 us; the launch traced here: 40.4 us
  Pallas kernels  38.9 us (96%)
  other arithmetic  0.89 us (2%)
  local copies, waits for them, and re-layouts  0.66 us (2%)
    pallas_call x1, Pallas kernels, on_device(): pl.pallas_call(kernel, out_shape=jax.ShapeDtypeStruct((ROWS, WIDTH), BF),...  38.9 us
    convert_element_type x1, other arithmetic, on_device(): return (normed.astype(F32) * out_gain[None, :]).astype(BF)  0.89 us

profile of v7, /device:TPU:1, one launch (start us, length us, event | category | flops | bytes accessed | tf_op | source)
XLA Modules:
  0.0 40.4 jit_solution(16488287777609799643)
XLA Ops:
  0.0 0.0 copy-start
  0.0 0.7 %copy-done = f32[4]{0:T(128)S(1)} copy-done((f32[4]{0:T(128)S(1)}, f32[4]{0:T(128)}, u32[]{:S(2)}) %copy-start) | copy-done | bytes 40
  0.7 0.0 copy-start.1
  0.7 38.9 %shard_map.55 = bf16[512,512]{1,0:T(8,128)(2,1)S(1)} custom-call(bf16[512,512]{1,0:T(8,128)(2,1)} %q_hbm.1, bf16[512,512]{1,0:T(8,128)(2,1)} %k_hbm.1, bf16[512,512]{1,0:T(8,128)(2,1)} %v_hbm.1, f32[4]{0:T(128)S(1)} %copy-done), custom_call_target="tpu_custom_call" | custom-call | tf_op jit(solution)/shard_map/pallas_call | solution.py:465
  39.5 0.0 copy-done.1
  39.6 0.9 %multiply_convert_fusion = bf16[512,512]{1,0:T(8,128)(2,1)} fusion(bf16[512,512]{1,0:T(8,128)(2,1)S(1)} %shard_map.55, f32[512]{0:T(512)S(1)} %copy-done.1), kind=kLoop, calls=%fused_computation | loop fusion | flops 786432 | bytes 1050624 | tf_op jit(solution)/shard_map/convert_element_type | solution.py:512
Async XLA Ops:
  0.0 0.7 %copy-start = (f32[4]{0:T(128)S(1)}, f32[4]{0:T(128)}, u32[]{:S(2)}) copy-start(f32[4]{0:T(128)} %scale_hbm.1) | copy-start | bytes 52
  0.7 38.9 %copy-start.1 = (f32[512]{0:T(512)S(1)}, f32[512]{0:T(512)}, u32[]{:S(2)}) copy-start(f32[512]{0:T(512)} %param.9) | copy-start | bytes 6148

commit v8 on v6

--- a/solution.py
+++ b/solution.py
@@ -119,15 +119,16 @@
     def signal(seq, head):
         pl.semaphore_signal(bar, inc=1, device_id=(seq, head), device_id_type=MESH)
 
-    for j in range(1, 8):
-        signal(at(x, (z + j) % NZ), me)
-        signal(d, (me + j) % NHEAD)
     for i in range(4):
         signal(at(x_back, 4 * s + i), me)
         signal(at(x_with, 4 * s + i), me)
         signal(at(x_far, 4 * s + i), me)
+    for j in (4, 3, 5, 2, 6, 1, 7):
+        signal(at(x, (z + j) % NZ), me)
     signal(left, me)
     signal(right, me)
+    for j in (4, 3, 5, 2, 6, 1, 7):
+        signal(d, (me + j) % NHEAD)
 
     loads = [
         pltpu.make_async_copy(src, dst, load.at[n])

time: 40.6 us -> 40.6 us (level)
  no operation moved by 1% of the time
where the time goes in v8:
time: 40.6 us; the launch traced here: 40.5 us
  Pallas kernels  38.9 us (96%)
  other arithmetic  0.89 us (2%)
  local copies, waits for them, and re-layouts  0.66 us (2%)
    pallas_call x1, Pallas kernels, on_device(): pl.pallas_call(kernel, out_shape=jax.ShapeDtypeStruct((ROWS, WIDTH), BF),...  38.9 us
    convert_element_type x1, other arithmetic, on_device(): return (normed.astype(F32) * out_gain[None, :]).astype(BF)  0.89 us

profile of v8, /device:TPU:1, one launch (start us, length us, event | category | flops | bytes accessed | tf_op | source)
XLA Modules:
  0.0 40.5 jit_solution(2239027911549307802)
XLA Ops:
  0.0 0.0 copy-start
  0.0 0.7 %copy-done = f32[4]{0:T(128)S(1)} copy-done((f32[4]{0:T(128)S(1)}, f32[4]{0:T(128)}, u32[]{:S(2)}) %copy-start) | copy-done | bytes 40
  0.7 0.0 copy-start.1
  0.7 38.9 %shard_map.55 = bf16[512,512]{1,0:T(8,128)(2,1)S(1)} custom-call(bf16[512,512]{1,0:T(8,128)(2,1)} %q_hbm.1, bf16[512,512]{1,0:T(8,128)(2,1)} %k_hbm.1, bf16[512,512]{1,0:T(8,128)(2,1)} %v_hbm.1, f32[4]{0:T(128)S(1)} %copy-done), custom_call_target="tpu_custom_call" | custom-call | tf_op jit(solution)/shard_map/pallas_call | solution.py:469
  39.6 0.0 copy-done.1
  39.6 0.9 %multiply_convert_fusion = bf16[512,512]{1,0:T(8,128)(2,1)} fusion(bf16[512,512]{1,0:T(8,128)(2,1)S(1)} %shard_map.55, f32[512]{0:T(512)S(1)} %copy-done.1), kind=kLoop, calls=%fused_computation | loop fusion | flops 786432 | bytes 1050624 | tf_op jit(solution)/shard_map/convert_element_type | solution.py:516
Async XLA Ops:
  0.0 0.7 %copy-start = (f32[4]{0:T(128)S(1)}, f32[4]{0:T(128)}, u32[]{:S(2)}) copy-start(f32[4]{0:T(128)} %scale_hbm.1) | copy-start | bytes 52
  0.7 38.9 %copy-start.1 = (f32[512]{0:T(512)S(1)}, f32[512]{0:T(512)}, u32[]{:S(2)}) copy-start(f32[512]{0:T(512)} %param.9) | copy-start | bytes 6148
